TPU v7x, 256 devices: a whole 4x4x8 slice. The times are simulated.
256 devices in a mesh: tmpl: 16 (over z, core), sta: 16 (over y, x).
Axes of the slice: x: 4, y: 4, z: 8, core: 2. Of those that a mesh axis runs over, the one named last changes fastest.
Arguments:
- waveforms: float32 [512, 3, 8192], P('sta', None, 'tmpl'), may hold values from -450 to 450
- templates: bfloat16 [512, 128, 450], P('sta', 'tmpl'), may hold values from -40 to 40
- pair_rows: int32 [512, 128], P('sta', 'tmpl'), may hold values from 0 to 4096, as said below
Outputs:
- detection: float32 [4096, 8192], P(('tmpl', 'sta'))
Inputs may be any that keep to these rules, and one draw needn't show every extreme that they name: Slot j of template block b at station s is pair_rows[s, b * 8 + j]. In each block the live slots come first and hold detection rows; the rest hold 4096. A block's live count is at most 8, and in every block some station has all 8 slots live. The rows of one station are distinct. A row r has home region (r // 16) % 16, and only stations of regions h - 1, h and h + 1 (taken cyclically, region of station s = s // 32) carry a row of home region h.
All inputs are finite; a program needn't handle non-finite values.
Results may differ from a plain program's by a relative error of at most 0.0065.
Values may be sent and summed in bfloat16 or wider, within the bound.
A program may use at most 64 MiB of HBM per device.

v0:
```python
import jax
import jax.numpy as jnp
from jax import lax
from jax.sharding import PartitionSpec as P

ROWS_DEV = 16


epsilon = 1e-06


def passed_along(x, axis, by):
    devices = lax.axis_size(axis)
    pairs = [(i, i + by) for i in range(devices) if 0 <= i + by < devices]
    return lax.ppermute(x, axis, pairs)


def extended_2(x, sides, width):
    for axis, dim in sides:
        devices, length = (lax.axis_size(axis), x.shape[dim])
        up = [(i, (i + 1) % devices) for i in range(devices)]
        down = [(j, i) for i, j in up]
        last = lax.slice_in_dim(x, length - width, length, axis=dim)
        first = lax.slice_in_dim(x, 0, width, axis=dim)
        before = lax.ppermute(last, axis, up)
        after = lax.ppermute(first, axis, down)
        x = jnp.concatenate([before, x, after], axis=dim)
    return x


def windows(extended, length, template_len):
    return jnp.stack(
        [extended[:, :, sample : sample + length] for sample in range(template_len)], axis=2
    )


def onehot_add(running, selector, correlation):
    first = correlation.astype(jnp.bfloat16)
    rest = correlation - first.astype(jnp.float32)
    second = rest.astype(jnp.bfloat16)
    third = (rest - second.astype(jnp.float32)).astype(jnp.bfloat16)
    total = jnp.dot(selector, first, preferred_element_type=jnp.float32)
    total = total + jnp.dot(selector, second, preferred_element_type=jnp.float32)
    total = total + jnp.dot(selector, third, preferred_element_type=jnp.float32)
    return running + total


def on_device(waveforms, templates, pair_rows):
    stations, channels, length = waveforms.shape
    window_size = templates.shape[2]
    template_len = window_size // channels
    n_tmpl = lax.axis_size("tmpl")
    n_sta = lax.axis_size("sta")
    row_group = ROWS_DEV * n_sta
    total_rows = row_group * n_tmpl
    region = lax.axis_index("sta")
    station_span = 8
    local_rows = n_tmpl * 3 * ROWS_DEV
    coarse = waveforms.astype(jnp.bfloat16)
    trailing = passed_along(coarse[:, :, : template_len - 1], "tmpl", -1)
    extended = jnp.concatenate([coarse, trailing], axis=2)
    squared = extended.astype(jnp.float32)
    squared = jnp.sum(squared * squared, axis=1)
    energy = squared[:, 0:length]
    for sample in range(1, template_len):
        energy = energy + squared[:, sample : sample + length]
    data_scale_all = lax.rsqrt(energy / window_size + epsilon)

    def locate(row_ids):
        occupied = row_ids < total_rows
        group_id = row_ids // row_group
        home_region = row_ids // ROWS_DEV % n_sta
        within = row_ids % ROWS_DEV
        relative = (home_region - region + 1 + n_sta) % n_sta
        slot_index = (group_id * 3 + relative) * ROWS_DEV + within
        return jnp.where(occupied, slot_index, local_rows)

    row_line = jnp.arange(local_rows, dtype=jnp.int32)

    def station_step(position, partial_value):
        offset = position * station_span
        segment = lax.dynamic_slice_in_dim(extended, offset, station_span, 0)
        hankel = windows(segment, length, template_len).reshape(station_span, window_size, length)
        data_scale = lax.dynamic_slice_in_dim(data_scale_all, offset, station_span, 0)
        own_waves = lax.dynamic_slice_in_dim(templates, offset, station_span, 0)
        own_rows = lax.dynamic_slice_in_dim(pair_rows, offset, station_span, 0)
        template_set = lax.all_gather(own_waves, "tmpl", axis=1, tiled=True)
        row_ids = lax.all_gather(own_rows, "tmpl", axis=1, tiled=True)
        squares = template_set.astype(jnp.float32)
        wave_scale = lax.rsqrt(jnp.mean(squares * squares, axis=2) + epsilon)
        product = jnp.einsum(
            "spk,skl->spl", template_set, hankel, preferred_element_type=jnp.float32
        )
        correlation = product * (wave_scale / window_size)[:, :, None] * data_scale[:, None, :]
        slot_index = locate(row_ids).reshape(-1)
        selector = (row_line[:, None] == slot_index[None, :]).astype(jnp.bfloat16)
        return onehot_add(partial_value, selector, correlation.reshape(-1, length))

    partial_value = lax.fori_loop(
        0, stations // station_span, station_step, jnp.zeros((local_rows, length), jnp.float32)
    )
    neighbours = partial_value.reshape(n_tmpl, 3, ROWS_DEV, length)
    arrived = lax.all_to_all(neighbours, "tmpl", split_axis=0, concat_axis=3, tiled=True)
    padded = extended_2(arrived, (("sta", 1),), 1)
    summed = padded[:, 0] + padded[:, 2] + padded[:, 4]
    return summed.reshape(ROWS_DEV, n_tmpl * length)


def solution(mesh):
    in_specs = (P("sta", None, "tmpl"), P("sta", "tmpl", None), P("sta", "tmpl"))
    out_specs = P(("tmpl", "sta"), None)
    return jax.shard_map(
        on_device, mesh=mesh, in_specs=in_specs, out_specs=out_specs, check_vma=False
    )
```

profile of v0, /device:TPU:1, one launch (start us, length us, event | category | flops | bytes accessed | tf_op | source)
XLA Modules:
  0.0 691.0 jit_solution(606933696909620708)
XLA Ops:
  0.0 0.9 convert_element_type.75
  1.0 5.1 collective-permute-start
  6.1 1.5 collective-permute-done
  7.7 2.6 fusion.180
  10.3 618.7 %while.17 = (s32[]{:T(128)}, f32[768,512]{1,0:T(8,128)}, s32[32,8]{0,1:T(8,128)S(1)}, s32[]{:T(128)}, bf16[32,8,450]{2,1,0:T(8,128)(2,1)}, /*index=5*/bf16[32,3,...) while((s32[]{:T(128)}, f32[768,512]{1,0:T(8,128)}, ...), condition=%wide.region_3.4_spmd.clone, body=%wide.region_1.3_spmd.clone.sunk | while | flops 2898398208 | bytes 36120324 | solution.py:99
  59.4 0.7 constant_dynamic-update-slice_fusion.371
  89.8 0.7 constant_dynamic-update-slice_fusion.415
  114.0 0.8 constant_dynamic-slice_fusion.156
  114.9 21.6 %all_gather.26 = bf16[8,128,450]{2,1,0:T(8,128)(2,1)S(1)} all-gather(bf16[8,8,450]{2,1,0:T(8,128)(2,1)S(1)} %constant_dynamic-slice_fusion.156), channel_id=1, replica_groups=mesh['tmpl'=16,'sta'=16] {'tmpl'}, dimensions={1}, use_global_device_ids=true | all-gather | bytes 979200 | tf_op jit(solution)/shard_map/while/body/eval_jaxpr/all_gather | solution.py:87
  136.8 4.4 multiply_multiply_fusion.2
  141.1 1.3 fusion.200
  142.5 14.7 %all_gather.27 = s32[8,128]{0,1:T(8,128)S(1)} all-gather(s32[8,8]{0,1:T(8,128)S(1)} %constant_dynamic-slice_fusion.158), channel_id=1, replica_groups=mesh['tmpl'=16,'sta'=16] {'tmpl'}, dimensions={1}, use_global_device_ids=true | all-gather | bytes 4352 | tf_op jit(solution)/shard_map/while/body/eval_jaxpr/all_gather | solution.py:88
  157.3 3.4 fusion.203
  160.7 2.1 fusion.202
  162.9 4.1 select_add_fusion.2
  215.9 0.7 constant_dynamic-update-slice_fusion.371
  227.0 0.7 constant_dynamic-update-slice_fusion.387
  270.5 0.8 constant_dynamic-slice_fusion.156
  271.3 18.6 %all_gather.26 = bf16[8,128,450]{2,1,0:T(8,128)(2,1)S(1)} all-gather(bf16[8,8,450]{2,1,0:T(8,128)(2,1)S(1)} %constant_dynamic-slice_fusion.156), channel_id=1, replica_groups=mesh['tmpl'=16,'sta'=16] {'tmpl'}, dimensions={1}, use_global_device_ids=true | all-gather | bytes 979200 | tf_op jit(solution)/shard_map/while/body/eval_jaxpr/all_gather | solution.py:87
  290.3 4.4 multiply_multiply_fusion.2
  294.7 1.3 fusion.200
  296.0 14.7 %all_gather.27 = s32[8,128]{0,1:T(8,128)S(1)} all-gather(s32[8,8]{0,1:T(8,128)S(1)} %constant_dynamic-slice_fusion.158), channel_id=1, replica_groups=mesh['tmpl'=16,'sta'=16] {'tmpl'}, dimensions={1}, use_global_device_ids=true | all-gather | bytes 4352 | tf_op jit(solution)/shard_map/while/body/eval_jaxpr/all_gather | solution.py:88
  310.8 3.4 fusion.203
  314.2 2.1 fusion.202
  316.5 4.5 select_add_fusion.2
  369.9 0.7 constant_dynamic-update-slice_fusion.371
  424.5 0.8 constant_dynamic-slice_fusion.156
  425.4 18.6 %all_gather.26 = bf16[8,128,450]{2,1,0:T(8,128)(2,1)S(1)} all-gather(bf16[8,8,450]{2,1,0:T(8,128)(2,1)S(1)} %constant_dynamic-slice_fusion.156), channel_id=1, replica_groups=mesh['tmpl'=16,'sta'=16] {'tmpl'}, dimensions={1}, use_global_device_ids=true | all-gather | bytes 979200 | tf_op jit(solution)/shard_map/while/body/eval_jaxpr/all_gather | solution.py:87
  444.3 4.4 multiply_multiply_fusion.2
  448.7 1.3 fusion.200
  450.1 14.7 %all_gather.27 = s32[8,128]{0,1:T(8,128)S(1)} all-gather(s32[8,8]{0,1:T(8,128)S(1)} %constant_dynamic-slice_fusion.158), channel_id=1, replica_groups=mesh['tmpl'=16,'sta'=16] {'tmpl'}, dimensions={1}, use_global_device_ids=true | all-gather | bytes 4352 | tf_op jit(solution)/shard_map/while/body/eval_jaxpr/all_gather | solution.py:88
  464.9 3.4 fusion.203
  468.2 2.1 fusion.202
  470.5 4.5 select_add_fusion.2
  523.9 0.7 constant_dynamic-update-slice_fusion.371
  578.5 0.8 constant_dynamic-slice_fusion.156
  579.4 18.7 %all_gather.26 = bf16[8,128,450]{2,1,0:T(8,128)(2,1)S(1)} all-gather(bf16[8,8,450]{2,1,0:T(8,128)(2,1)S(1)} %constant_dynamic-slice_fusion.156), channel_id=1, replica_groups=mesh['tmpl'=16,'sta'=16] {'tmpl'}, dimensions={1}, use_global_device_ids=true | all-gather | bytes 979200 | tf_op jit(solution)/shard_map/while/body/eval_jaxpr/all_gather | solution.py:87
  598.4 4.4 multiply_multiply_fusion.2
  602.7 1.3 fusion.200
  604.1 14.7 %all_gather.27 = s32[8,128]{0,1:T(8,128)S(1)} all-gather(s32[8,8]{0,1:T(8,128)S(1)} %constant_dynamic-slice_fusion.158), channel_id=1, replica_groups=mesh['tmpl'=16,'sta'=16] {'tmpl'}, dimensions={1}, use_global_device_ids=true | all-gather | bytes 4352 | tf_op jit(solution)/shard_map/while/body/eval_jaxpr/all_gather | solution.py:88
  618.9 3.4 fusion.203
  622.2 2.1 fusion.202
  624.5 4.5 select_add_fusion.2
  629.0 44.6 %all_to_all.18 = f32[16,3,16,512]{3,2,1,0:T(8,128)S(1)} all-to-all(f32[16,3,16,512]{3,2,1,0:T(8,128)} %bitcast.1245), channel_id=1, replica_groups=mesh['tmpl'=16,'sta'=16] {'tmpl'}, dimensions={0} | all-to-all | bytes 3145728 | tf_op jit(solution)/shard_map/all_to_all | solution.py:103
  673.8 1.3 collective-permute-start.1
  675.1 3.8 collective-permute-start.2
  678.9 11.2 %collective-permute-done.1 = f32[1,1,16,8192]{3,2,1,0:T(8,128)S(1)} collective-permute-done((f32[1,1,16,8192]{3,2,1,0:T(8,128)S(1)}, f32[1,1,16,8192]{3,2,1,0:T(8,128)S(1)}, u32[]{:S(2)}, u32[]{:S(2)}) %collective-permute-start.1) | collective-permute-done | bytes 524320 | tf_op jit(solution)/shard_map/ppermute | solution.py:25
  690.2 0.9 fusion.177
  (631 shorter events, 412.1 us)
Async XLA Ops:
  1.0 6.7 collective-permute-start
  7.7 2.6 copy-start
  673.8 16.3 %collective-permute-start.1 = (f32[1,1,16,8192]{3,2,1,0:T(8,128)S(1)}, f32[1,1,16,8192]{3,2,1,0:T(8,128)S(1)}, u32[]{:S(2)}, u32[]{:S(2)}) collective-permute-start(f32[1,1,16,8192]{3,2,1,0:T(8,128)S(1)} %get-tuple-element.290), channel_id=1, source_target_pairs={{0,1},{1,2},{2,3},{3,4},{4,5},{5,6},{6,7},{7,8},{8,9},{9,10},{10,1... | collective-permute-start | bytes 1572872 | tf_op jit(solution)/shard_map/ppermute | solution.py:25
  675.1 15.1 %collective-permute-start.2 = (f32[1,1,16,8192]{3,2,1,0:T(8,128)S(1)}, f32[1,1,16,8192]{3,2,1,0:T(8,128)S(1)}, u32[]{:S(2)}, u32[]{:S(2)}) collective-permute-start(f32[1,1,16,8192]{3,2,1,0:T(8,128)S(1)} %get-tuple-element.291), channel_id=1, source_target_pairs={{1,0},{2,1},{3,2},{4,3},{5,4},{6,5},{7,6},{8,7},{9,8},{10,9},{11,1... | collective-permute-start | bytes 1572872 | tf_op jit(solution)/shard_map/ppermute | solution.py:26
where the time goes:
time: 692 us; the launch traced here: 691 us
  local copies, waits for them, and re-layouts  418 us (60%)
  blocking collectives  181 us (26%)
  matrix products  57.2 us (8%)
  waiting for transfers between devices  12.8 us (2%)
  other arithmetic  11.3 us (2%)
  starting transfers between devices  10.2 us (1%)
    while x596, local copies, waits for them, and re-layouts  411 us
    all_gather x4, blocking collectives, station_step(): template_set = lax.all_gather(own_waves, 'tmpl', axis=1, tiled=True)  77.5 us
    all_gather x4, blocking collectives, station_step(): row_ids = lax.all_gather(own_rows, 'tmpl', axis=1, tiled=True)  58.8 us
    all_to_all x1, blocking collectives, on_device(): lax.all_to_all(neighbours, 'tmpl', split_axis=0, concat_axis=3, tiled=True)  44.6 us
    dot_general x4, matrix products, onehot_add(): total = jnp.dot(selector, first, preferred_element_type=jnp.float32)  17.7 us
    dot_general x4, matrix products, station_step(): jnp.einsum('spk,skl->spl', template_set, hankel, preferred_element_type=j...  17.5 us
  transfers between devices with their start and end apart: 3, of which 2 were waited for; matrix products, arithmetic and copies ran while one was open for 0% of the time, Pallas kernels for 0%

commit v1 on v0

v1 whole, which is shorter than its diff:
```python
import functools

import jax
import jax.numpy as jnp
from jax import lax
from jax.experimental import pallas as pl
from jax.experimental.pallas import tpu as pltpu
from jax.sharding import PartitionSpec as P

TLEN = 150
WINDOW = 450
EPS = 1e-06
CAP = 8
ROWS_DEV = 16
STATIONS = 32
HALF = 16
LAGS = 512
WIDE = 768
DEPTH = 512
SLOTS = 128
CHUNKS = 8
SPAN = HALF // CHUNKS
CHIPS = 8
BLOCKS = 16
REGIONS = 16
FAR = 4
PIECES = 4
PIECE = 256 // PIECES
MESH = pl.DeviceIdType.MESH


def kernel(
    waves_ref, own_ref, out_ref,
    bank, hankel, shifts, wave, mate, halo_out, halo_in, scale_ref, corr, rows_ref, total,
    outgo, income, part, gathered,
    mate_sem, halo_sem, ring_send, ring_recv, share_send, share_recv, side_send, side_recv,
    spread_send, spread_recv,
):
    block = lax.axis_index("tmpl")
    region = lax.axis_index("sta")
    z = block // 2
    core = block % 2
    other = 1 - core

    def at(chip, which):
        return (lax.rem(chip + CHIPS, CHIPS) * 2 + which, region)

    barrier = pltpu.get_barrier_semaphore()

    @pl.loop(1, BLOCKS)
    def _(step):
        pl.semaphore_signal(
            barrier, inc=1, device_id=(lax.rem(block + step, BLOCKS), region), device_id_type=MESH
        )

    for side in (1, REGIONS - 1):
        pl.semaphore_signal(
            barrier, inc=1, device_id=(block, lax.rem(region + side, REGIONS)), device_id_type=MESH
        )

    coarse = waves_ref[...].astype(jnp.bfloat16)
    halo_out[...] = coarse[:, :256]
    for tile in range(4):
        wave[tile] = coarse[:, tile * 128 : tile * 128 + 128].astype(jnp.float32)
    pl.semaphore_wait(barrier, BLOCKS + 1)

    to_mate = pltpu.make_async_remote_copy(
        src_ref=own_ref.at[pl.ds(pl.multiple_of(other * 128, 128), 128)],
        dst_ref=mate,
        send_sem=mate_sem.at[0],
        recv_sem=mate_sem.at[1],
        device_id=at(z, other),
        device_id_type=MESH,
    )
    to_mate.start()
    to_left = pltpu.make_async_remote_copy(
        src_ref=halo_out,
        dst_ref=halo_in,
        send_sem=halo_sem.at[0],
        recv_sem=halo_sem.at[1],
        device_id=(lax.rem(block + BLOCKS - 1, BLOCKS), region),
        device_id_type=MESH,
    )
    to_left.start()

    total[...] = jnp.zeros_like(total)

    def place(who, chunk, chip):
        first = pl.multiple_of(who * HALF + chunk * SPAN, SPAN)
        chip = lax.rem(chip + CHIPS, CHIPS)
        return bank.at[pl.ds(first, SPAN), pl.ds(pl.multiple_of(chip * 16, 16), 16), :]

    def ring(way, chunk, hop, origin):
        ref = place(core, chunk, origin)
        return pltpu.make_async_remote_copy(
            src_ref=ref,
            dst_ref=ref,
            send_sem=ring_send.at[way, chunk, hop],
            recv_sem=ring_recv.at[way, chunk, hop],
            device_id=at(z + (1 if way == 0 else -1), core),
            device_id_type=MESH,
        )

    def share(who, chunk, away, chip):
        ref = place(who, chunk, chip)
        return pltpu.make_async_remote_copy(
            src_ref=ref,
            dst_ref=ref,
            send_sem=share_send.at[chunk, away],
            recv_sem=share_recv.at[chunk, away],
            device_id=at(z, other),
            device_id_type=MESH,
        )

    to_mate.wait()
    for pair in range(HALF // 2):
        mine = own_ref[pl.ds(pl.multiple_of(core * 128 + pair * 16, 16), 16), :].astype(jnp.float32)
        theirs = mate[pl.ds(pair * 16, 16), :].astype(jnp.float32)
        low = jnp.where(core == 0, mine, theirs)
        high = jnp.where(core == 0, theirs, mine)
        for i in range(2):
            both = jnp.concatenate([low[8 * i : 8 * i + 8], high[8 * i : 8 * i + 8]], axis=0)
            bank[core * HALF + pair * 2 + i, pl.ds(pl.multiple_of(z * 16, 16), 16), :] = both.astype(
                jnp.bfloat16
            )

    def waves_ready():
        to_left.wait()
        last = jnp.where(block == BLOCKS - 1, 0.0, 1.0)
        for tile in range(2):
            one = halo_in[:, tile * 128 : tile * 128 + 128]
            wave[4 + tile] = one.astype(jnp.float32) * last
        every = jnp.concatenate([wave[tile] for tile in range(6)], axis=1)
        for lane in range(16):
            moved = every if lane == 0 else pltpu.roll(every, WIDE - lane, 1)
            for tile in range(6):
                shifts[tile, pl.ds(lane, 96, stride=16), :] = moved[:, tile * 128 : tile * 128 + 128]
        pieces = []
        for tile in range(6):
            squared = jnp.zeros((STATIONS, 128), jnp.float32)
            for channel in range(3):
                one = wave[tile, pl.ds(channel, STATIONS, stride=3), :]
                squared = squared + one * one
            pieces.append(squared)
        squared = jnp.concatenate(pieces, axis=1)
        def left(x, by):
            return pltpu.roll(x, WIDE - by, 1)
        two = squared + left(squared, 1)
        four = two + left(two, 2)
        run = four
        for by in (4, 8):
            run = run + left(run, by)
        sixteen = run
        for by in (16, 32, 64):
            run = run + left(run, by)
        run = run + left(sixteen, 128) + left(four, 144) + left(two, 148)
        scale_ref[...] = lax.rsqrt(run[:, :LAGS] / WINDOW + EPS)

    lower = lax.broadcasted_iota(jnp.int32, (16, LAGS), 0)

    def build(station):
        rolled = []
        for c in range(3):
            rows = pl.ds(pl.multiple_of((station * 3 + c) * 16, 16), 16)
            every = jnp.concatenate([shifts[tile, rows, :] for tile in range(6)], axis=1)
            rolled.append(every.astype(jnp.bfloat16))

        def taken(channel, start):
            if start >= 0:
                return rolled[channel][:, start : start + LAGS]
            return pltpu.roll(rolled[channel].astype(jnp.float32), -start, 1)[:, :LAGS].astype(jnp.bfloat16)

        for tile in range(DEPTH // 16):
            first = tile * 16
            if first >= WINDOW:
                value = jnp.zeros((16, LAGS), jnp.bfloat16)
            else:
                channel, start = divmod(first, TLEN)
                value = taken(channel, start)
                rest = TLEN - start
                if rest < 16:
                    if channel < 2:
                        after = taken(channel + 1, start - TLEN)
                    else:
                        after = jnp.zeros((16, LAGS), jnp.bfloat16)
                    value = jnp.where(lower < rest, value, after)
            hankel[station, pl.ds(first, 16), :] = value

    ids = lax.broadcasted_iota(jnp.int32, (16, SLOTS), 1)
    picker = jnp.where(ids == WINDOW - 384, 64.0, jnp.where(ids == WINDOW + 1 - 384, 1.0, 0.0))
    picker = picker.astype(jnp.bfloat16)
    live = lax.broadcasted_iota(jnp.int32, (SLOTS, DEPTH), 1) < WINDOW

    def correlate(station, where):
        waves = bank[station]
        product = jnp.dot(waves, hankel[station], preferred_element_type=jnp.float32)
        wide = jnp.where(live, waves.astype(jnp.float32), 0.0)
        power = jnp.sum(wide * wide, axis=1, keepdims=True)
        factor = lax.rsqrt(power / WINDOW + EPS) / WINDOW
        value = product * factor * scale_ref[pl.ds(station, 1), :]
        start = pl.multiple_of(where * SLOTS, SLOTS)
        corr[pl.ds(start, SLOTS), :] = value.astype(jnp.bfloat16)
        row = lax.dot_general(
            picker, waves[:, 384:], (((1,), (1,)), ((), ())), preferred_element_type=jnp.float32
        )
        row = row[:8].astype(jnp.int32)
        group = row >> 8
        home = (row >> 4) & 15
        relative = (home - region + 1 + REGIONS) & 15
        apart = ((group >> 1) - z + CHIPS) & 7
        order = jnp.where(apart >= 4, 2 * apart - 8, 7 - 2 * apart)
        index = relative * 256 + (order * 2 + (group & 1)) * ROWS_DEV + (row & 15)
        index = jnp.where(row < 4096, index, 4096)
        rows_ref[where] = index

    across = lax.broadcasted_iota(jnp.int32, (256, SLOTS), 0)

    def scatter(relative):
        picks = []
        for i in range(2 * SPAN):
            index = rows_ref[i][:1, :]
            picks.append((across + relative * 256 == index).astype(jnp.bfloat16))
        selector = jnp.concatenate(picks, axis=1)
        start = pl.multiple_of(relative * 256, 256)
        total[pl.ds(start, 256), :] += jnp.dot(
            selector, corr[...], preferred_element_type=jnp.float32
        )

    def hops_of(way):
        return range(FAR)

    def moves(turn):
        for hop in range(FAR):
            chunk = turn - 1 - hop
            inside = (chunk >= 0) & (chunk < CHUNKS)
            for way in range(2):
                sign = -1 if way == 0 else 1
                arrives = inside
                if hop == FAR - 1:
                    arrives = inside & (lax.rem(chunk + CHUNKS, 2) == way)

                @pl.when(arrives)
                def _():
                    origin = z + sign * (hop + 1)
                    ring(way, chunk, hop, origin).wait_recv()
                    away = hop + 1 if way == 0 else CHIPS - 1 - hop
                    if hop + 1 < FAR - 1:
                        ring(way, chunk, hop + 1, origin).start()
                    elif hop + 1 == FAR - 1:

                        @pl.when(lax.rem(chunk, 2) == way)
                        def _():
                            ring(way, chunk, hop + 1, origin).start()

                    share(core, chunk, away, origin).start()

        @pl.when(turn < CHUNKS)
        def _():
            for way in range(2):
                ring(way, turn, 0, z).start()
            share(core, turn, 0, z).start()

    @pl.loop(0, CHUNKS + FAR)
    def _(turn):
        moves(turn)

        @pl.when(turn == 0)
        def _():
            waves_ready()

        @pl.when(turn < FAR)
        def _():
            @pl.loop(0, STATIONS // FAR)
            def _(i):
                build(turn * (STATIONS // FAR) + i)

        @pl.when(turn >= FAR)
        def _():
            chunk = turn - FAR

            @pl.loop(0, SPAN)
            def _(i):
                correlate(core * HALF + chunk * SPAN + i, i)

            @pl.loop(0, CHIPS)
            def _(away):
                share(other, chunk, away, z).wait_recv()

            @pl.loop(0, SPAN)
            def _(i):
                correlate(other * HALF + chunk * SPAN + i, SPAN + i)

            @pl.when(turn < CHUNKS + FAR - 1)
            def _():
                @pl.loop(0, 3)
                def _(relative):
                    scatter(relative)

    def side(direction, piece):
        step = REGIONS - 1 if direction == 0 else 1
        span = pl.ds(piece * PIECE, PIECE)
        return pltpu.make_async_remote_copy(
            src_ref=outgo.at[direction, span],
            dst_ref=income.at[direction, span],
            send_sem=side_send.at[direction, piece],
            recv_sem=side_recv.at[direction, piece],
            device_id=(block, lax.rem(region + step, REGIONS)),
            device_id_type=MESH,
        )

    for direction in range(2):
        scatter(2 * direction)
        outgo[direction] = total[pl.ds(512 * direction, 256), :].astype(jnp.bfloat16)
        for piece in range(PIECES):
            side(direction, piece).start()
    scatter(1)

    def spread(piece, slot):
        order = piece * 2 + slot // 2
        apart = 4 + order // 2 if order % 2 == 0 else 3 - order // 2
        return order, apart, slot % 2

    def send_out(order, apart, which):
        rows = pl.ds((order * 2 + which) * ROWS_DEV, ROWS_DEV)
        return pltpu.make_async_remote_copy(
            src_ref=part.at[rows],
            dst_ref=gathered.at[block],
            send_sem=spread_send.at[order * 2 + which],
            recv_sem=spread_recv.at[block],
            device_id=at(z + apart, which),
            device_id_type=MESH,
        )

    for piece in range(PIECES):
        for direction in range(2):
            side(direction, piece).wait_recv()
        span = pl.ds(piece * PIECE, PIECE)
        summed = total[pl.ds(256 + piece * PIECE, PIECE), :]
        summed = summed + income[0, span].astype(jnp.float32) + income[1, span].astype(jnp.float32)
        part[span] = summed.astype(jnp.bfloat16)
        for slot in range(4):
            order, apart, which = spread(piece, slot)
            if apart == 0:

                @pl.when(core != which)
                def _():
                    send_out(order, apart, which).start()

            else:
                send_out(order, apart, which).start()

    here = pl.ds(pl.multiple_of((14 + core) * ROWS_DEV, ROWS_DEV), ROWS_DEV)
    gathered[block] = part[here]

    @pl.loop(0, CHUNKS)
    def _(chunk):
        for way in range(2):
            for hop in range(FAR - 1):
                ring(way, chunk, hop, z).wait_send()

            @pl.when(lax.rem(chunk, 2) == way)
            def _():
                ring(way, chunk, FAR - 1, z).wait_send()

        @pl.loop(0, CHIPS)
        def _(away):
            share(core, chunk, away, z).wait_send()

    for direction in range(2):
        for piece in range(PIECES):
            side(direction, piece).wait_send()

    def spread_wait(source):
        return pltpu.make_async_remote_copy(
            src_ref=part.at[pl.ds(0, ROWS_DEV)],
            dst_ref=gathered.at[source],
            send_sem=spread_send.at[0],
            recv_sem=spread_recv.at[source],
            device_id=(block, region),
            device_id_type=MESH,
        )

    for piece in range(PIECES):
        for slot in range(4):
            order, apart, which = spread(piece, slot)
            if apart == 0:

                @pl.when(core != which)
                def _():
                    send_out(order, apart, which).wait_send()

            else:
                send_out(order, apart, which).wait_send()

    @pl.loop(1, BLOCKS)
    def _(step):
        spread_wait(lax.rem(block + step, BLOCKS)).wait_recv()

    for source in range(BLOCKS):
        out_ref[:, pl.ds(source * LAGS, LAGS)] = gathered[source]


def on_device(waveforms, templates, pair_rows):
    waves = waveforms.reshape(STATIONS * 3, LAGS)
    number = jnp.stack([pair_rows >> 6, pair_rows & 63], axis=2).astype(jnp.bfloat16)
    fill = jnp.zeros((STATIONS, CAP, DEPTH - WINDOW - 2), jnp.bfloat16)
    own = jnp.concatenate([templates, number, fill], axis=2).reshape(STATIONS * CAP, DEPTH)
    bf16, f32 = jnp.bfloat16, jnp.float32
    dma = pltpu.SemaphoreType.DMA
    result = pl.pallas_call(
        kernel,
        out_shape=jax.ShapeDtypeStruct((ROWS_DEV, BLOCKS * LAGS), bf16),
        in_specs=[pl.BlockSpec(memory_space=pltpu.VMEM)] * 2,
        out_specs=pl.BlockSpec(memory_space=pltpu.VMEM),
        scratch_shapes=[
            pltpu.VMEM((STATIONS, SLOTS, DEPTH), bf16),
            pltpu.VMEM((STATIONS, DEPTH, LAGS), bf16),
            pltpu.VMEM((6, STATIONS * 3 * 16, 128), f32),
            pltpu.VMEM((6, STATIONS * 3, 128), f32),
            pltpu.VMEM((128, DEPTH), bf16),
            pltpu.VMEM((STATIONS * 3, 256), bf16),
            pltpu.VMEM((STATIONS * 3, 256), bf16),
            pltpu.VMEM((STATIONS, LAGS), f32),
            pltpu.VMEM((2 * SPAN * SLOTS, LAGS), bf16),
            pltpu.VMEM((2 * SPAN, 8, SLOTS), jnp.int32),
            pltpu.VMEM((768, LAGS), f32),
            pltpu.VMEM((2, 256, LAGS), bf16),
            pltpu.VMEM((2, 256, LAGS), bf16),
            pltpu.VMEM((256, LAGS), bf16),
            pltpu.VMEM((BLOCKS, ROWS_DEV, LAGS), bf16),
            dma((2,)),
            dma((2,)),
            dma((2, CHUNKS, FAR)),
            dma((2, CHUNKS, FAR)),
            dma((CHUNKS, CHIPS)),
            dma((CHUNKS, CHIPS)),
            dma((2, PIECES)),
            dma((2, PIECES)),
            dma((BLOCKS,)),
            dma((BLOCKS,)),
        ],
        compiler_params=pltpu.CompilerParams(
            collective_id=0, has_side_effects=True, vmem_limit_bytes=60 * 1024 * 1024
        ),
    )(waves, own)
    return result.astype(jnp.float32)


def solution(mesh):
    in_specs = (P("sta", None, "tmpl"), P("sta", "tmpl", None), P("sta", "tmpl"))
    out_specs = P(("tmpl", "sta"), None)
    return jax.shard_map(
        on_device, mesh=mesh, in_specs=in_specs, out_specs=out_specs, check_vma=False
    )
```

time: 692 us -> 85.2 us (0.12)
  local copies, waits for them, and re-layouts: 418 us -> 1.31 us
  blocking collectives: 181 us -> 0 us
  Pallas kernels: 0 us -> 79.4 us
  matrix products: 57.2 us -> 0 us
  waiting for transfers between devices: 12.8 us -> 0 us
  starting transfers between devices: 10.2 us -> 0 us
  other arithmetic: 11.3 us -> 4.27 us
    while x596 -> x0, local copies, waits for them, and re-layouts: 411 us -> none
    all_gather x8 -> x0, blocking collectives: 136 us -> none  [the longest x4 77.5 us: station_step(): template_set = lax.all_gather(own_waves, 'tmpl', axis=1, tiled=True)]
    pallas_call x0 -> x1, Pallas kernels: none -> 79.4 us  [on_device(): pl.pallas_call(kernel, out_shape=jax.ShapeDtypeStruct((ROWS_DEV, BLOCKS *...]
    dot_general x16 -> x0, matrix products: 57.2 us -> none  [the longest x4 17.7 us: onehot_add(): total = jnp.dot(selector, first, preferred_element_type=jnp.float32)]
    all_to_all x1 -> x0, blocking collectives: 44.6 us -> none  [on_device(): lax.all_to_all(neighbours, 'tmpl', split_axis=0, concat_axis=3, tiled=True)]
    ppermute x3 -> x0, waiting for transfers between devices: 12.8 us -> none  [the longest x1 11.2 us: extended_2(): before = lax.ppermute(last, axis, up)]
    ppermute x3 -> x0, starting transfers between devices: 10.2 us -> none  [the longest x1 5.15 us: passed_along(): return lax.ppermute(x, axis, pairs)]
  transfers between devices with their start and end apart: 3 -> 0, of which waited for: 2 -> 0; matrix products, arithmetic and copies ran while one was open for 0% -> 0% of each run, Pallas kernels for 0% -> 0%
where the time goes in v1:
time: 85.2 us; the launch traced here: 85 us
  Pallas kernels  79.4 us (93%)
  other arithmetic  4.27 us (5%)
  local copies, waits for them, and re-layouts  1.31 us (2%)
    pallas_call x1, Pallas kernels, on_device(): pl.pallas_call(kernel, out_shape=jax.ShapeDtypeStruct((ROWS_DEV, BLOCKS *...  79.4 us
    reshape x1, other arithmetic, on_device(): jnp.concatenate([templates, number, fill], axis=2)  1.8 us
    convert_element_type x1, other arithmetic, on_device(): return result.astype(jnp.float32)  1.78 us

profile of v1, /device:TPU:1, one launch (start us, length us, event | category | flops | bytes accessed | tf_op | source)
XLA Modules:
  0.0 85.0 jit_solution(12296713858090447475)
XLA Ops:
  0.0 0.1 pad.3.clone
  0.1 0.7 fusion
  0.8 0.2 copy.8
  0.9 0.2 copy.9
  1.1 0.0 copy-start
  1.1 1.8 %maximum_bitcast_fusion.own_ref = bf16[256,512]{1,0:T(8,128)(2,1)} fusion(bf16[32,8,1]{2,1,0:T(8,128)(2,1)S(1)} %copy.9, bf16[32,8,1]{2,1,0:T(8,128)(2,1)S(1)} %copy.8, bf16[32,8,450]{2,1,0:T(8,128)(2,1)} %param.4, bf16[512]{0:T(512)(128)(2,1)S(1)} %pad.3.clone), kind=kLoop, calls=%fused_computation | loop fusion | flops 1048576 | bytes 494592 | tf_op jit(solution)/shard_map/reshape | solution.py:407
  2.9 0.0 copy-done
  2.9 0.1 copy.7
  3.0 0.8 reshape.6.waves_ref
  3.8 79.4 %shard_map.37 = bf16[16,8192]{1,0:T(8,128)(2,1)} custom-call(f32[96,512]{1,0:T(8,128)} %reshape.6.waves_ref, bf16[256,512]{1,0:T(8,128)(2,1)} %maximum_bitcast_fusion.own_ref), custom_call_target="tpu_custom_call" | custom-call | tf_op jit(solution)/shard_map/pallas_call | solution.py:410
  83.2 1.8 %convert_element_type.4 = f32[16,8192]{1,0:T(8,128)} convert(bf16[16,8192]{1,0:T(8,128)(2,1)} %shard_map.37) | non-fusion elementwise | flops 131072 | bytes 786432 | tf_op jit(solution)/shard_map/convert_element_type | solution.py:446
  (1 shorter events, 0.0 us)
Async XLA Ops:
  1.1 1.8 %copy-start = (f32[32,3,512]{2,0,1:T(8,128)S(1)}, f32[32,3,512]{2,0,1:T(8,128)}, u32[]{:S(2)}) copy-start(f32[32,3,512]{2,0,1:T(8,128)} %param.3) | copy-start | bytes 589828

commit v2 on v1

--- a/solution.py
+++ b/solution.py
@@ -13,13 +13,13 @@
 CAP = 8
 ROWS_DEV = 16
 STATIONS = 32
-HALF = 16
 LAGS = 512
 WIDE = 768
 DEPTH = 512
 SLOTS = 128
 CHUNKS = 8
-SPAN = HALF // CHUNKS
+SPAN = STATIONS // CHUNKS
+AHEAD = 3
 CHIPS = 8
 BLOCKS = 16
 REGIONS = 16
@@ -30,10 +30,10 @@
 
 
 def kernel(
-    waves_ref, own_ref, out_ref,
-    bank, hankel, shifts, wave, mate, halo_out, halo_in, scale_ref, corr, rows_ref, total,
+    waves_ref, own_ref, number_ref, out_ref,
+    bank, hankel, shifts, wave, halo_out, halo_in, scale_ref, corr, rows_ref, total,
     outgo, income, part, gathered,
-    mate_sem, halo_sem, ring_send, ring_recv, share_send, share_recv, side_send, side_recv,
+    halo_sem, ring_send, ring_recv, share_send, share_recv, side_send, side_recv,
     spread_send, spread_recv,
 ):
     block = lax.axis_index("tmpl")
@@ -46,33 +46,33 @@
         return (lax.rem(chip + CHIPS, CHIPS) * 2 + which, region)
 
     barrier = pltpu.get_barrier_semaphore()
-
-    @pl.loop(1, BLOCKS)
-    def _(step):
-        pl.semaphore_signal(
-            barrier, inc=1, device_id=(lax.rem(block + step, BLOCKS), region), device_id_type=MESH
-        )
-
-    for side in (1, REGIONS - 1):
-        pl.semaphore_signal(
-            barrier, inc=1, device_id=(block, lax.rem(region + side, REGIONS)), device_id_type=MESH
-        )
+    near = [at(z, other), at(z + 1, core), at(z - 1, core), at(z + 2 * core - 1, other)]
+    near += [(block, lax.rem(region + side, REGIONS)) for side in (1, REGIONS - 1)]
+    for device in near:
+        pl.semaphore_signal(barrier, inc=1, device_id=device, device_id_type=MESH)
 
     coarse = waves_ref[...].astype(jnp.bfloat16)
     halo_out[...] = coarse[:, :256]
     for tile in range(4):
         wave[tile] = coarse[:, tile * 128 : tile * 128 + 128].astype(jnp.float32)
-    pl.semaphore_wait(barrier, BLOCKS + 1)
-
-    to_mate = pltpu.make_async_remote_copy(
-        src_ref=own_ref.at[pl.ds(pl.multiple_of(other * 128, 128), 128)],
-        dst_ref=mate,
-        send_sem=mate_sem.at[0],
-        recv_sem=mate_sem.at[1],
-        device_id=at(z, other),
-        device_id_type=MESH,
-    )
-    to_mate.start()
+
+    station = lax.broadcasted_iota(jnp.int32, (STATIONS * CAP, STATIONS), 0) >> 3
+    expand = (station == lax.broadcasted_iota(jnp.int32, (STATIONS * CAP, STATIONS), 1))
+    expand = expand.astype(jnp.bfloat16)
+    mine = lax.broadcasted_iota(jnp.int32, (STATIONS * CAP, CAP), 0) & 7
+    mine = mine == lax.broadcasted_iota(jnp.int32, (STATIONS * CAP, CAP), 1)
+    lane = lax.broadcasted_iota(jnp.int32, (STATIONS * CAP, 128), 1)
+    numbers = jnp.zeros((STATIONS * CAP, 128), jnp.float32)
+    for i, digits in enumerate((number_ref[...] >> 6, number_ref[...] & 63)):
+        digits = digits.astype(jnp.float32).astype(jnp.bfloat16)
+        column = jnp.dot(expand, digits, preferred_element_type=jnp.float32)
+        column = jnp.sum(jnp.where(mine, column, 0.0), axis=1, keepdims=True)
+        numbers = jnp.where(lane == WINDOW - 384 + i, column, numbers)
+    bank[block, :, :384] = own_ref[:, :384]
+    bank[block, :, 384:] = numbers.astype(jnp.bfloat16)
+    bank[block, :, 384:WINDOW] = own_ref[:, 384:]
+    pl.semaphore_wait(barrier, len(near))
+
     to_left = pltpu.make_async_remote_copy(
         src_ref=halo_out,
         dst_ref=halo_in,
@@ -83,46 +83,48 @@
     )
     to_left.start()
 
-    total[...] = jnp.zeros_like(total)
-
-    def place(who, chunk, chip):
-        first = pl.multiple_of(who * HALF + chunk * SPAN, SPAN)
-        chip = lax.rem(chip + CHIPS, CHIPS)
-        return bank.at[pl.ds(first, SPAN), pl.ds(pl.multiple_of(chip * 16, 16), 16), :]
+    def place(chunk, chip, which):
+        first = pl.multiple_of(chunk * SPAN * CAP, SPAN * CAP)
+        return bank.at[lax.rem(chip + CHIPS, CHIPS) * 2 + which, pl.ds(first, SPAN * CAP), :]
 
     def ring(way, chunk, hop, origin):
-        ref = place(core, chunk, origin)
+        ref = place(chunk, origin, core)
         return pltpu.make_async_remote_copy(
             src_ref=ref,
             dst_ref=ref,
-            send_sem=ring_send.at[way, chunk, hop],
+            send_sem=ring_send,
             recv_sem=ring_recv.at[way, chunk, hop],
             device_id=at(z + (1 if way == 0 else -1), core),
             device_id_type=MESH,
         )
 
-    def share(who, chunk, away, chip):
-        ref = place(who, chunk, chip)
+    def share(chunk, chip):
+        ref = place(chunk, chip, core)
         return pltpu.make_async_remote_copy(
             src_ref=ref,
             dst_ref=ref,
-            send_sem=share_send.at[chunk, away],
-            recv_sem=share_recv.at[chunk, away],
+            send_sem=share_send,
+            recv_sem=share_recv.at[chunk],
             device_id=at(z, other),
             device_id_type=MESH,
         )
 
-    to_mate.wait()
-    for pair in range(HALF // 2):
-        mine = own_ref[pl.ds(pl.multiple_of(core * 128 + pair * 16, 16), 16), :].astype(jnp.float32)
-        theirs = mate[pl.ds(pair * 16, 16), :].astype(jnp.float32)
-        low = jnp.where(core == 0, mine, theirs)
-        high = jnp.where(core == 0, theirs, mine)
-        for i in range(2):
-            both = jnp.concatenate([low[8 * i : 8 * i + 8], high[8 * i : 8 * i + 8]], axis=0)
-            bank[core * HALF + pair * 2 + i, pl.ds(pl.multiple_of(z * 16, 16), 16), :] = both.astype(
-                jnp.bfloat16
-            )
+    def bulk(count, send, receive):
+        ref = bank.at[pl.ds(0, count // CHUNKS)]
+        return pltpu.make_async_remote_copy(
+            src_ref=ref, dst_ref=ref, send_sem=send, recv_sem=receive,
+            device_id=at(z, other), device_id_type=MESH,
+        )
+
+    def inject(chunk):
+        for way in range(2):
+            ring(way, chunk, 0, z).start()
+        share(chunk, z).start()
+
+    for chunk in range(AHEAD + 1):
+        inject(chunk)
+
+    total[...] = jnp.zeros_like(total)
 
     def waves_ready():
         to_left.wait()
@@ -162,18 +164,17 @@
         rolled = []
         for c in range(3):
             rows = pl.ds(pl.multiple_of((station * 3 + c) * 16, 16), 16)
-            every = jnp.concatenate([shifts[tile, rows, :] for tile in range(6)], axis=1)
-            rolled.append(every.astype(jnp.bfloat16))
+            rolled.append(jnp.concatenate([shifts[tile, rows, :] for tile in range(6)], axis=1))
 
         def taken(channel, start):
-            if start >= 0:
-                return rolled[channel][:, start : start + LAGS]
-            return pltpu.roll(rolled[channel].astype(jnp.float32), -start, 1)[:, :LAGS].astype(jnp.bfloat16)
+            if start == 0:
+                return rolled[channel][:, :LAGS]
+            return pltpu.roll(rolled[channel], (WIDE - start) % WIDE, 1)[:, :LAGS]
 
         for tile in range(DEPTH // 16):
             first = tile * 16
             if first >= WINDOW:
-                value = jnp.zeros((16, LAGS), jnp.bfloat16)
+                value = jnp.zeros((16, LAGS), jnp.float32)
             else:
                 channel, start = divmod(first, TLEN)
                 value = taken(channel, start)
@@ -182,20 +183,30 @@
                     if channel < 2:
                         after = taken(channel + 1, start - TLEN)
                     else:
-                        after = jnp.zeros((16, LAGS), jnp.bfloat16)
+                        after = jnp.zeros((16, LAGS), jnp.float32)
                     value = jnp.where(lower < rest, value, after)
-            hankel[station, pl.ds(first, 16), :] = value
+            hankel[station, pl.ds(first, 16), :] = value.astype(jnp.bfloat16)
 
     ids = lax.broadcasted_iota(jnp.int32, (16, SLOTS), 1)
     picker = jnp.where(ids == WINDOW - 384, 64.0, jnp.where(ids == WINDOW + 1 - 384, 1.0, 0.0))
     picker = picker.astype(jnp.bfloat16)
-    live = lax.broadcasted_iota(jnp.int32, (SLOTS, DEPTH), 1) < WINDOW
-
-    def correlate(station, where):
-        waves = bank[station]
+    live = lax.broadcasted_iota(jnp.int32, (SLOTS, 128), 1) < WINDOW - 384
+
+    def correlate(pair, where):
+        rows = pl.ds(pl.multiple_of(pair * 16, 16), 16)
+        both = [bank[b, rows, :].astype(jnp.float32) for b in range(BLOCKS)]
+        for i in range(2):
+            one(pair * 2 + i, where * 2 + i, [x[i * 8 : i * 8 + 8] for x in both])
+
+    def one(station, where, pieces):
+        wide = jnp.concatenate(pieces, axis=0)
+        waves = wide.astype(jnp.bfloat16)
         product = jnp.dot(waves, hankel[station], preferred_element_type=jnp.float32)
-        wide = jnp.where(live, waves.astype(jnp.float32), 0.0)
-        power = jnp.sum(wide * wide, axis=1, keepdims=True)
+        last = jnp.where(live, wide[:, 384:], 0.0)
+        power = last * last
+        for tile in range(3):
+            power = power + wide[:, tile * 128 : tile * 128 + 128] * wide[:, tile * 128 : tile * 128 + 128]
+        power = jnp.sum(power, axis=1, keepdims=True)
         factor = lax.rsqrt(power / WINDOW + EPS) / WINDOW
         value = product * factor * scale_ref[pl.ds(station, 1), :]
         start = pl.multiple_of(where * SLOTS, SLOTS)
@@ -217,7 +228,7 @@
 
     def scatter(relative):
         picks = []
-        for i in range(2 * SPAN):
+        for i in range(SPAN):
             index = rows_ref[i][:1, :]
             picks.append((across + relative * 256 == index).astype(jnp.bfloat16))
         selector = jnp.concatenate(picks, axis=1)
@@ -225,9 +236,6 @@
         total[pl.ds(start, 256), :] += jnp.dot(
             selector, corr[...], preferred_element_type=jnp.float32
         )
-
-    def hops_of(way):
-        return range(FAR)
 
     def moves(turn):
         for hop in range(FAR):
@@ -243,7 +251,6 @@
                 def _():
                     origin = z + sign * (hop + 1)
                     ring(way, chunk, hop, origin).wait_recv()
-                    away = hop + 1 if way == 0 else CHIPS - 1 - hop
                     if hop + 1 < FAR - 1:
                         ring(way, chunk, hop + 1, origin).start()
                     elif hop + 1 == FAR - 1:
@@ -252,13 +259,16 @@
                         def _():
                             ring(way, chunk, hop + 1, origin).start()
 
-                    share(core, chunk, away, origin).start()
-
-        @pl.when(turn < CHUNKS)
+                    share(chunk, origin).start()
+
+        @pl.when((turn >= 1) & (turn + AHEAD < CHUNKS))
         def _():
-            for way in range(2):
-                ring(way, turn, 0, z).start()
-            share(core, turn, 0, z).start()
+            inject(turn + AHEAD)
+
+    def spots(chunk):
+        @pl.loop(0, SPAN // 2)
+        def _(i):
+            correlate(chunk * (SPAN // 2) + i, i)
 
     @pl.loop(0, CHUNKS + FAR)
     def _(turn):
@@ -274,27 +284,17 @@
             def _(i):
                 build(turn * (STATIONS // FAR) + i)
 
+        @pl.when(turn > FAR)
+        def _():
+            @pl.loop(0, 3)
+            def _(relative):
+                scatter(relative)
+
         @pl.when(turn >= FAR)
         def _():
             chunk = turn - FAR
-
-            @pl.loop(0, SPAN)
-            def _(i):
-                correlate(core * HALF + chunk * SPAN + i, i)
-
-            @pl.loop(0, CHIPS)
-            def _(away):
-                share(other, chunk, away, z).wait_recv()
-
-            @pl.loop(0, SPAN)
-            def _(i):
-                correlate(other * HALF + chunk * SPAN + i, SPAN + i)
-
-            @pl.when(turn < CHUNKS + FAR - 1)
-            def _():
-                @pl.loop(0, 3)
-                def _(relative):
-                    scatter(relative)
+            bulk(CHUNKS, share_send, share_recv.at[chunk]).wait_recv()
+            spots(chunk)
 
     def side(direction, piece):
         step = REGIONS - 1 if direction == 0 else 1
@@ -352,20 +352,8 @@
     here = pl.ds(pl.multiple_of((14 + core) * ROWS_DEV, ROWS_DEV), ROWS_DEV)
     gathered[block] = part[here]
 
-    @pl.loop(0, CHUNKS)
-    def _(chunk):
-        for way in range(2):
-            for hop in range(FAR - 1):
-                ring(way, chunk, hop, z).wait_send()
-
-            @pl.when(lax.rem(chunk, 2) == way)
-            def _():
-                ring(way, chunk, FAR - 1, z).wait_send()
-
-        @pl.loop(0, CHIPS)
-        def _(away):
-            share(core, chunk, away, z).wait_send()
-
+    bulk(CHUNKS * 7, ring_send, share_recv.at[0]).wait_send()
+    bulk(CHUNKS * 8, share_send, share_recv.at[0]).wait_send()
     for direction in range(2):
         for piece in range(PIECES):
             side(direction, piece).wait_send()
@@ -402,38 +390,34 @@
 
 def on_device(waveforms, templates, pair_rows):
     waves = waveforms.reshape(STATIONS * 3, LAGS)
-    number = jnp.stack([pair_rows >> 6, pair_rows & 63], axis=2).astype(jnp.bfloat16)
-    fill = jnp.zeros((STATIONS, CAP, DEPTH - WINDOW - 2), jnp.bfloat16)
-    own = jnp.concatenate([templates, number, fill], axis=2).reshape(STATIONS * CAP, DEPTH)
+    own = templates.reshape(STATIONS * CAP, WINDOW)
     bf16, f32 = jnp.bfloat16, jnp.float32
     dma = pltpu.SemaphoreType.DMA
     result = pl.pallas_call(
         kernel,
         out_shape=jax.ShapeDtypeStruct((ROWS_DEV, BLOCKS * LAGS), bf16),
-        in_specs=[pl.BlockSpec(memory_space=pltpu.VMEM)] * 2,
+        in_specs=[pl.BlockSpec(memory_space=pltpu.VMEM)] * 3,
         out_specs=pl.BlockSpec(memory_space=pltpu.VMEM),
         scratch_shapes=[
-            pltpu.VMEM((STATIONS, SLOTS, DEPTH), bf16),
+            pltpu.VMEM((BLOCKS, STATIONS * CAP, DEPTH), bf16),
             pltpu.VMEM((STATIONS, DEPTH, LAGS), bf16),
             pltpu.VMEM((6, STATIONS * 3 * 16, 128), f32),
             pltpu.VMEM((6, STATIONS * 3, 128), f32),
-            pltpu.VMEM((128, DEPTH), bf16),
             pltpu.VMEM((STATIONS * 3, 256), bf16),
             pltpu.VMEM((STATIONS * 3, 256), bf16),
             pltpu.VMEM((STATIONS, LAGS), f32),
-            pltpu.VMEM((2 * SPAN * SLOTS, LAGS), bf16),
-            pltpu.VMEM((2 * SPAN, 8, SLOTS), jnp.int32),
+            pltpu.VMEM((SPAN * SLOTS, LAGS), bf16),
+            pltpu.VMEM((SPAN, 8, SLOTS), jnp.int32),
             pltpu.VMEM((768, LAGS), f32),
             pltpu.VMEM((2, 256, LAGS), bf16),
             pltpu.VMEM((2, 256, LAGS), bf16),
             pltpu.VMEM((256, LAGS), bf16),
             pltpu.VMEM((BLOCKS, ROWS_DEV, LAGS), bf16),
             dma((2,)),
-            dma((2,)),
+            dma,
             dma((2, CHUNKS, FAR)),
-            dma((2, CHUNKS, FAR)),
-            dma((CHUNKS, CHIPS)),
-            dma((CHUNKS, CHIPS)),
+            dma,
+            dma((CHUNKS,)),
             dma((2, PIECES)),
             dma((2, PIECES)),
             dma((BLOCKS,)),
@@ -442,7 +426,7 @@
         compiler_params=pltpu.CompilerParams(
             collective_id=0, has_side_effects=True, vmem_limit_bytes=60 * 1024 * 1024
         ),
-    )(waves, own)
+    )(waves, own, pair_rows)
     return result.astype(jnp.float32)
 
 

time: 85.2 us -> 70.8 us (0.83)
  Pallas kernels: 79.4 us -> 65.7 us
  other arithmetic: 4.27 us -> 1.78 us
  local copies, waits for them, and re-layouts: 1.31 us -> 3.2 us
    pallas_call x1, Pallas kernels: 79.4 us -> 65.7 us  [on_device(): pl.pallas_call(kernel, out_shape=jax.ShapeDtypeStruct((ROWS_DEV, BLOCKS *...]
    unnamed x3 -> x2, local copies, waits for them, and re-layouts: 0.14 us -> 2.42 us
    reshape x1 -> x0, other arithmetic: 1.8 us -> none  [on_device(): jnp.concatenate([templates, number, fill], axis=2)]
where the time goes in v2:
time: 70.8 us; the launch traced here: 70.7 us
  Pallas kernels  65.7 us (93%)
  local copies, waits for them, and re-layouts  3.2 us (5%)
  other arithmetic  1.78 us (3%)
    pallas_call x1, Pallas kernels, on_device(): pl.pallas_call(kernel, out_shape=jax.ShapeDtypeStruct((ROWS_DEV, BLOCKS *...  65.7 us
    unnamed x2, local copies, waits for them, and re-layouts  2.42 us
    convert_element_type x1, other arithmetic, on_device(): return result.astype(jnp.float32)  1.78 us

profile of v2, /device:TPU:1, one launch (start us, length us, event | category | flops | bytes accessed | tf_op | source)
XLA Modules:
  0.0 70.7 jit_solution(8246045764944418403)
XLA Ops:
  0.0 1.4 %copy.7.number_ref = s32[32,8]{1,0:T(8,128)} copy(s32[32,8]{0,1:T(8,128)} %param.5) | data formatting | bytes 2048 | tf_op args[2]
  1.4 1.1 %copy.6 = f32[32,3,512]{2,1,0:T(4,128)S(1)} copy(f32[32,3,512]{2,0,1:T(8,128)} %param.3) | data formatting | bytes 393216 | tf_op args[0]
  2.4 0.8 %reshape.6.waves_ref = f32[96,512]{1,0:T(8,128)} reshape(f32[32,3,512]{2,1,0:T(4,128)S(1)} %copy.6) | data formatting | bytes 393216 | tf_op jit(solution)/shard_map/reshape | solution.py:392
  3.2 65.7 %shard_map.37 = bf16[16,8192]{1,0:T(8,128)(2,1)} custom-call(f32[96,512]{1,0:T(8,128)} %reshape.6.waves_ref, bf16[256,450]{1,0:T(8,128)(2,1)} %bitcast.1, s32[32,8]{1,0:T(8,128)} %copy.7.number_ref), custom_call_target="tpu_custom_call" | custom-call | tf_op jit(solution)/shard_map/pallas_call | solution.py:396
  68.9 1.8 %convert_element_type.3 = f32[16,8192]{1,0:T(8,128)} convert(bf16[16,8192]{1,0:T(8,128)(2,1)} %shard_map.37) | non-fusion elementwise | flops 131072 | bytes 786432 | tf_op jit(solution)/shard_map/convert_element_type | solution.py:430

commit v3 on v2

--- a/solution.py
+++ b/solution.py
@@ -56,11 +56,11 @@
     for tile in range(4):
         wave[tile] = coarse[:, tile * 128 : tile * 128 + 128].astype(jnp.float32)
 
-    station = lax.broadcasted_iota(jnp.int32, (STATIONS * CAP, STATIONS), 0) >> 3
-    expand = (station == lax.broadcasted_iota(jnp.int32, (STATIONS * CAP, STATIONS), 1))
+    slot = lax.broadcasted_iota(jnp.int32, (STATIONS * CAP, CAP), 0) & 7
+    expand = slot == lax.broadcasted_iota(jnp.int32, (STATIONS * CAP, CAP), 1)
     expand = expand.astype(jnp.bfloat16)
-    mine = lax.broadcasted_iota(jnp.int32, (STATIONS * CAP, CAP), 0) & 7
-    mine = mine == lax.broadcasted_iota(jnp.int32, (STATIONS * CAP, CAP), 1)
+    mine = lax.broadcasted_iota(jnp.int32, (STATIONS * CAP, STATIONS), 0) >> 3
+    mine = mine == lax.broadcasted_iota(jnp.int32, (STATIONS * CAP, STATIONS), 1)
     lane = lax.broadcasted_iota(jnp.int32, (STATIONS * CAP, 128), 1)
     numbers = jnp.zeros((STATIONS * CAP, 128), jnp.float32)
     for i, digits in enumerate((number_ref[...] >> 6, number_ref[...] & 63)):
@@ -141,7 +141,7 @@
         for tile in range(6):
             squared = jnp.zeros((STATIONS, 128), jnp.float32)
             for channel in range(3):
-                one = wave[tile, pl.ds(channel, STATIONS, stride=3), :]
+                one = wave[tile, pl.ds(channel * STATIONS, STATIONS), :]
                 squared = squared + one * one
             pieces.append(squared)
         squared = jnp.concatenate(pieces, axis=1)
@@ -163,7 +163,7 @@
     def build(station):
         rolled = []
         for c in range(3):
-            rows = pl.ds(pl.multiple_of((station * 3 + c) * 16, 16), 16)
+            rows = pl.ds(pl.multiple_of((c * STATIONS + station) * 16, 16), 16)
             rolled.append(jnp.concatenate([shifts[tile, rows, :] for tile in range(6)], axis=1))
 
         def taken(channel, start):
@@ -224,15 +224,18 @@
         index = jnp.where(row < 4096, index, 4096)
         rows_ref[where] = index
 
-    across = lax.broadcasted_iota(jnp.int32, (256, SLOTS), 0)
+    across = lax.broadcasted_iota(jnp.int32, (256, SLOTS), 0).astype(jnp.float32).astype(jnp.bfloat16)
 
     def scatter(relative):
         picks = []
         for i in range(SPAN):
-            index = rows_ref[i][:1, :]
-            picks.append((across + relative * 256 == index).astype(jnp.bfloat16))
+            index = rows_ref[i] - relative * 256
+            index = jnp.where((index >= 0) & (index < 256), index, 512)
+            index = index.astype(jnp.float32).astype(jnp.bfloat16)
+            same = across == jnp.broadcast_to(index[:1], (256, SLOTS))
+            picks.append(jnp.where(same, jnp.bfloat16(1), jnp.bfloat16(0)))
         selector = jnp.concatenate(picks, axis=1)
-        start = pl.multiple_of(relative * 256, 256)
+        start = relative * 256
         total[pl.ds(start, 256), :] += jnp.dot(
             selector, corr[...], preferred_element_type=jnp.float32
         )
@@ -266,8 +269,7 @@
             inject(turn + AHEAD)
 
     def spots(chunk):
-        @pl.loop(0, SPAN // 2)
-        def _(i):
+        for i in range(SPAN // 2):
             correlate(chunk * (SPAN // 2) + i, i)
 
     @pl.loop(0, CHUNKS + FAR)
@@ -278,16 +280,15 @@
         def _():
             waves_ready()
 
-        @pl.when(turn < FAR)
+        @pl.when(turn < CHUNKS)
         def _():
-            @pl.loop(0, STATIONS // FAR)
+            @pl.loop(0, SPAN)
             def _(i):
-                build(turn * (STATIONS // FAR) + i)
+                build(turn * SPAN + i)
 
         @pl.when(turn > FAR)
         def _():
-            @pl.loop(0, 3)
-            def _(relative):
+            for relative in range(3):
                 scatter(relative)
 
         @pl.when(turn >= FAR)
@@ -389,7 +390,7 @@
 
 
 def on_device(waveforms, templates, pair_rows):
-    waves = waveforms.reshape(STATIONS * 3, LAGS)
+    waves = waveforms.transpose(1, 0, 2).reshape(STATIONS * 3, LAGS)
     own = templates.reshape(STATIONS * CAP, WINDOW)
     bf16, f32 = jnp.bfloat16, jnp.float32
     dma = pltpu.SemaphoreType.DMA
@@ -426,7 +427,7 @@
         compiler_params=pltpu.CompilerParams(
             collective_id=0, has_side_effects=True, vmem_limit_bytes=60 * 1024 * 1024
         ),
-    )(waves, own, pair_rows)
+    )(waves, own, pair_rows.T)
     return result.astype(jnp.float32)
 
 

time: 70.8 us -> 65.8 us (0.929)
  local copies, waits for them, and re-layouts: 3.2 us -> 0 us
  Pallas kernels: 65.7 us -> 63.9 us
    unnamed x2 -> x0, local copies, waits for them, and re-layouts: 2.42 us -> none
    pallas_call x1, Pallas kernels: 65.7 us -> 63.9 us  [on_device(): pl.pallas_call(kernel, out_shape=jax.ShapeDtypeStruct((ROWS_DEV, BLOCKS *...]
    reshape x1 -> x0, local copies, waits for them, and re-layouts: 0.78 us -> none  [on_device(): waves = waveforms.reshape(STATIONS * 3, LAGS)]
where the time goes in v3:
time: 65.8 us; the launch traced here: 65.7 us
  Pallas kernels  63.9 us (97%)
  other arithmetic  1.78 us (3%)
    pallas_call x1, Pallas kernels, on_device(): pl.pallas_call(kernel, out_shape=jax.ShapeDtypeStruct((ROWS_DEV, BLOCKS *...  63.9 us
    convert_element_type x1, other arithmetic, on_device(): return result.astype(jnp.float32)  1.78 us

profile of v3, /device:TPU:1, one launch (start us, length us, event | category | flops | bytes accessed | tf_op | source)
XLA Modules:
  0.0 65.7 jit_solution(1547350102410541938)
XLA Ops:
  0.0 63.9 %shard_map.37 = bf16[16,8192]{1,0:T(8,128)(2,1)} custom-call(f32[96,512]{1,0:T(8,128)} %bitcast.6, bf16[256,450]{1,0:T(8,128)(2,1)} %bitcast.5, s32[8,32]{1,0:T(8,128)} %bitcast.7), custom_call_target="tpu_custom_call" | custom-call | tf_op jit(solution)/shard_map/pallas_call | solution.py:397
  63.9 1.8 %convert_element_type.3 = f32[16,8192]{1,0:T(8,128)} convert(bf16[16,8192]{1,0:T(8,128)(2,1)} %shard_map.37) | non-fusion elementwise | flops 131072 | bytes 786432 | tf_op jit(solution)/shard_map/convert_element_type | solution.py:431

commit v4 on v3

--- a/solution.py
+++ b/solution.py
@@ -24,6 +24,9 @@
 BLOCKS = 16
 REGIONS = 16
 FAR = 4
+WHEN = (1, 4, 7, 10)
+READY = WHEN[-1] + 1
+TICKS = READY + 2 * (CHUNKS - 1)
 PIECES = 4
 PIECE = 256 // PIECES
 MESH = pl.DeviceIdType.MESH
@@ -31,10 +34,10 @@
 
 def kernel(
     waves_ref, own_ref, number_ref, out_ref,
-    bank, hankel, shifts, wave, halo_out, halo_in, scale_ref, corr, rows_ref, total,
+    bank, extra, last_tile, hankel, shifts, wave, halo_out, halo_in, scale_ref, corr, rows_ref, total,
     outgo, income, part, gathered,
-    halo_sem, ring_send, ring_recv, share_send, share_recv, side_send, side_recv,
-    spread_send, spread_recv,
+    halo_sem, ring_send, ring_recv, share_send, share_recv, extra_send, extra_recv, extra_share,
+    side_send, side_recv, spread_send, spread_recv,
 ):
     block = lax.axis_index("tmpl")
     region = lax.axis_index("sta")
@@ -51,26 +54,38 @@
     for device in near:
         pl.semaphore_signal(barrier, inc=1, device_id=device, device_id_type=MESH)
 
+    lane8 = lax.broadcasted_iota(jnp.int32, (CAP, 128), 1)
     coarse = waves_ref[...].astype(jnp.bfloat16)
     halo_out[...] = coarse[:, :256]
     for tile in range(4):
         wave[tile] = coarse[:, tile * 128 : tile * 128 + 128].astype(jnp.float32)
 
-    slot = lax.broadcasted_iota(jnp.int32, (STATIONS * CAP, CAP), 0) & 7
-    expand = slot == lax.broadcasted_iota(jnp.int32, (STATIONS * CAP, CAP), 1)
-    expand = expand.astype(jnp.bfloat16)
-    mine = lax.broadcasted_iota(jnp.int32, (STATIONS * CAP, STATIONS), 0) >> 3
-    mine = mine == lax.broadcasted_iota(jnp.int32, (STATIONS * CAP, STATIONS), 1)
-    lane = lax.broadcasted_iota(jnp.int32, (STATIONS * CAP, 128), 1)
-    numbers = jnp.zeros((STATIONS * CAP, 128), jnp.float32)
+    last_tile[...] = jnp.zeros_like(last_tile)
+    last_tile[:, : WINDOW - 384] = own_ref[:, 384:].astype(jnp.float32)
+    for chunk in range(CHUNKS):
+        rows = pl.ds(chunk * SPAN * CAP, SPAN * CAP)
+        for tile in range(3):
+            bank[block, chunk, pl.ds(tile * SPAN * CAP, SPAN * CAP), :] = own_ref[
+                rows, tile * 128 : tile * 128 + 128
+            ]
+        ends = [last_tile[pl.ds((chunk * SPAN + i) * CAP, CAP), :] for i in range(SPAN)]
+        joined = [
+            jnp.where(lane8 < 64, ends[i], pltpu.roll(ends[i + 1], 64, 1)) for i in range(0, SPAN, 2)
+        ]
+        bank[block, chunk, pl.ds(3 * SPAN * CAP, SPAN * CAP // 2), :] = jnp.concatenate(
+            joined, axis=0
+        ).astype(jnp.bfloat16)
+    spread_lane = lax.broadcasted_iota(jnp.int32, (STATIONS, 128), 1)
+    spread_row = lax.broadcasted_iota(jnp.int32, (STATIONS, 128), 0)
+    extras = jnp.zeros((CAP, 128), jnp.float32)
     for i, digits in enumerate((number_ref[...] >> 6, number_ref[...] & 63)):
         digits = digits.astype(jnp.float32).astype(jnp.bfloat16)
-        column = jnp.dot(expand, digits, preferred_element_type=jnp.float32)
-        column = jnp.sum(jnp.where(mine, column, 0.0), axis=1, keepdims=True)
-        numbers = jnp.where(lane == WINDOW - 384 + i, column, numbers)
-    bank[block, :, :384] = own_ref[:, :384]
-    bank[block, :, 384:] = numbers.astype(jnp.bfloat16)
-    bank[block, :, 384:WINDOW] = own_ref[:, 384:]
+        selects = (spread_lane == spread_row * 4 + 2 + i).astype(jnp.bfloat16)
+        extras = extras + jnp.dot(digits, selects, preferred_element_type=jnp.float32)
+    for station in range(STATIONS):
+        moved = pltpu.roll(last_tile[pl.ds(station * CAP, CAP), :], (station * 4 + 64) % 128, 1)
+        extras = jnp.where((lane8 >> 1) == station * 2, moved, extras)
+    extra[block] = jnp.concatenate([extras, jnp.zeros_like(extras)], axis=0).astype(jnp.bfloat16)
     pl.semaphore_wait(barrier, len(near))
 
     to_left = pltpu.make_async_remote_copy(
@@ -83,46 +98,41 @@
     )
     to_left.start()
 
-    def place(chunk, chip, which):
-        first = pl.multiple_of(chunk * SPAN * CAP, SPAN * CAP)
-        return bank.at[lax.rem(chip + CHIPS, CHIPS) * 2 + which, pl.ds(first, SPAN * CAP), :]
-
-    def ring(way, chunk, hop, origin):
-        ref = place(chunk, origin, core)
-        return pltpu.make_async_remote_copy(
-            src_ref=ref,
-            dst_ref=ref,
-            send_sem=ring_send,
-            recv_sem=ring_recv.at[way, chunk, hop],
-            device_id=at(z + (1 if way == 0 else -1), core),
-            device_id_type=MESH,
-        )
-
-    def share(chunk, chip):
-        ref = place(chunk, chip, core)
-        return pltpu.make_async_remote_copy(
-            src_ref=ref,
-            dst_ref=ref,
-            send_sem=share_send,
-            recv_sem=share_recv.at[chunk],
-            device_id=at(z, other),
-            device_id_type=MESH,
-        )
-
-    def bulk(count, send, receive):
-        ref = bank.at[pl.ds(0, count // CHUNKS)]
+    def index_of(chip):
+        return lax.rem(chip + CHIPS, CHIPS) * 2 + core
+
+    def remote(ref, send, receive, device):
         return pltpu.make_async_remote_copy(
             src_ref=ref, dst_ref=ref, send_sem=send, recv_sem=receive,
-            device_id=at(z, other), device_id_type=MESH,
+            device_id=device, device_id_type=MESH,
         )
+
+    ahead = [at(z + 1, core), at(z - 1, core)]
+    mate = at(z, other)
+
+    def ring(way, chunk, hop, origin):
+        ref = bank.at[index_of(origin), chunk]
+        remote(ref, ring_send, ring_recv.at[chunk, hop], ahead[way]).start()
+
+    def share(chunk, chip):
+        remote(bank.at[index_of(chip), chunk], share_send, share_recv.at[chunk], mate).start()
+
+    def ring_extra(way, hop, origin):
+        remote(extra.at[index_of(origin)], extra_send, extra_recv.at[hop], ahead[way]).start()
+
+    def share_extra(chip):
+        remote(extra.at[index_of(chip)], extra_send, extra_share, mate).start()
 
     def inject(chunk):
         for way in range(2):
-            ring(way, chunk, 0, z).start()
-        share(chunk, z).start()
-
+            ring(way, chunk, 0, z)
+        share(chunk, z)
+
+    for way in range(2):
+        ring_extra(way, 0, z)
     for chunk in range(AHEAD + 1):
         inject(chunk)
+    share_extra(z)
 
     total[...] = jnp.zeros_like(total)
 
@@ -192,14 +202,26 @@
     picker = picker.astype(jnp.bfloat16)
     live = lax.broadcasted_iota(jnp.int32, (SLOTS, 128), 1) < WINDOW - 384
 
-    def correlate(pair, where):
-        rows = pl.ds(pl.multiple_of(pair * 16, 16), 16)
-        both = [bank[b, rows, :].astype(jnp.float32) for b in range(BLOCKS)]
+    lane_all = lax.broadcasted_iota(jnp.int32, (SLOTS, 128), 1)
+
+    def correlate(chunk, pair, slot):
+        tiles = []
+        for tile in range(3):
+            rows = pl.ds(pl.multiple_of(tile * SPAN * CAP + pair * 16, 16), 16)
+            tiles.append([bank[b, chunk, rows, :].astype(jnp.float32) for b in range(BLOCKS)])
+        rows = pl.ds(3 * SPAN * CAP, 16)
+        ends = [bank[b, chunk, rows, :].astype(jnp.float32) for b in range(BLOCKS)]
+        ends = jnp.concatenate([jnp.where(pair == 0, x[:8], x[8:]) for x in ends], axis=0)
+        extras = jnp.concatenate([extra[b].astype(jnp.float32)[:8] for b in range(BLOCKS)], axis=0)
         for i in range(2):
-            one(pair * 2 + i, where * 2 + i, [x[i * 8 : i * 8 + 8] for x in both])
-
-    def one(station, where, pieces):
-        wide = jnp.concatenate(pieces, axis=0)
+            station = chunk * SPAN + pair * 2 + i
+            end = ends if i == 0 else pltpu.roll(ends, 64, 1)
+            few = pltpu.roll(extras, lax.rem(192 - station * 4, 128), 1)
+            end = jnp.where(lane_all < 64, end, jnp.where(lane_all < 68, few, 0.0))
+            pieces = [jnp.concatenate([x[i * 8 : i * 8 + 8] for x in t], axis=0) for t in tiles]
+            one(station, slot, pair * 2 + i, jnp.concatenate(pieces + [end], axis=1))
+
+    def one(station, slot, where, wide):
         waves = wide.astype(jnp.bfloat16)
         product = jnp.dot(waves, hankel[station], preferred_element_type=jnp.float32)
         last = jnp.where(live, wide[:, 384:], 0.0)
@@ -210,7 +232,7 @@
         factor = lax.rsqrt(power / WINDOW + EPS) / WINDOW
         value = product * factor * scale_ref[pl.ds(station, 1), :]
         start = pl.multiple_of(where * SLOTS, SLOTS)
-        corr[pl.ds(start, SLOTS), :] = value.astype(jnp.bfloat16)
+        corr[slot, pl.ds(start, SLOTS), :] = value.astype(jnp.bfloat16)
         row = lax.dot_general(
             picker, waves[:, 384:], (((1,), (1,)), ((), ())), preferred_element_type=jnp.float32
         )
@@ -222,14 +244,14 @@
         order = jnp.where(apart >= 4, 2 * apart - 8, 7 - 2 * apart)
         index = relative * 256 + (order * 2 + (group & 1)) * ROWS_DEV + (row & 15)
         index = jnp.where(row < 4096, index, 4096)
-        rows_ref[where] = index
+        rows_ref[slot, where] = index
 
     across = lax.broadcasted_iota(jnp.int32, (256, SLOTS), 0).astype(jnp.float32).astype(jnp.bfloat16)
 
-    def scatter(relative):
+    def scatter(relative, slot):
         picks = []
         for i in range(SPAN):
-            index = rows_ref[i] - relative * 256
+            index = rows_ref[slot, i] - relative * 256
             index = jnp.where((index >= 0) & (index < 256), index, 512)
             index = index.astype(jnp.float32).astype(jnp.bfloat16)
             same = across == jnp.broadcast_to(index[:1], (256, SLOTS))
@@ -237,65 +259,107 @@
         selector = jnp.concatenate(picks, axis=1)
         start = relative * 256
         total[pl.ds(start, 256), :] += jnp.dot(
-            selector, corr[...], preferred_element_type=jnp.float32
+            selector, corr[slot], preferred_element_type=jnp.float32
         )
 
-    def moves(turn):
+    def pair_of(ref, count):
+        return ref.at[0, pl.ds(0, count)]
+
+    def moves(tick):
         for hop in range(FAR):
-            chunk = turn - 1 - hop
-            inside = (chunk >= 0) & (chunk < CHUNKS)
-            for way in range(2):
-                sign = -1 if way == 0 else 1
-                arrives = inside
-                if hop == FAR - 1:
-                    arrives = inside & (lax.rem(chunk + CHUNKS, 2) == way)
-
-                @pl.when(arrives)
-                def _():
-                    origin = z + sign * (hop + 1)
-                    ring(way, chunk, hop, origin).wait_recv()
+            late = tick - WHEN[hop]
+
+            @pl.when((late >= 0) & (late < 2 * CHUNKS) & (lax.rem(late + 2 * TICKS, 2) == 0))
+            def _():
+                chunk = lax.div(late, 2)
+                count = 2 if hop < FAR - 1 else 1
+                arrived = bank.at[0, pl.ds(0, count)]
+                remote(arrived, ring_send, ring_recv.at[chunk, hop], mate).wait_recv()
+                for way in range(2):
+                    origin = z + (-1 if way == 0 else 1) * (hop + 1)
                     if hop + 1 < FAR - 1:
-                        ring(way, chunk, hop + 1, origin).start()
+                        ring(way, chunk, hop + 1, origin)
+                        share(chunk, origin)
                     elif hop + 1 == FAR - 1:
 
                         @pl.when(lax.rem(chunk, 2) == way)
                         def _():
-                            ring(way, chunk, hop + 1, origin).start()
-
-                    share(chunk, origin).start()
-
-        @pl.when((turn >= 1) & (turn + AHEAD < CHUNKS))
+                            ring(way, chunk, hop + 1, origin)
+
+                        share(chunk, origin)
+                if hop == FAR - 1:
+                    share(chunk, z + FAR)
+
+            if hop < FAR - 1:
+
+                @pl.when(tick == WHEN[hop])
+                def _():
+                    remote(extra.at[pl.ds(0, 2)], extra_send, extra_recv.at[hop], mate).wait_recv()
+                    for way in range(2):
+                        origin = z + (-1 if way == 0 else 1) * (hop + 1)
+                        if hop + 1 < FAR - 1 or way == 0:
+                            ring_extra(way, hop + 1, origin)
+                        share_extra(origin)
+
+            else:
+
+                @pl.when(tick == WHEN[hop])
+                def _():
+                    remote(extra.at[0], extra_send, extra_recv.at[hop], mate).wait_recv()
+                    share_extra(z + FAR)
+
+        @pl.when((tick > 0) & (lax.rem(tick, 2) == 0) & (lax.div(tick, 2) + AHEAD < CHUNKS))
         def _():
-            inject(turn + AHEAD)
-
-    def spots(chunk):
-        for i in range(SPAN // 2):
-            correlate(chunk * (SPAN // 2) + i, i)
-
-    @pl.loop(0, CHUNKS + FAR)
-    def _(turn):
-        moves(turn)
-
-        @pl.when(turn == 0)
-        def _():
-            waves_ready()
-
-        @pl.when(turn < CHUNKS)
+            inject(lax.div(tick, 2) + AHEAD)
+
+    def shared(chunk):
+        remote(bank.at[pl.ds(0, CHIPS), 0], share_send, share_recv.at[chunk], mate).wait_recv()
+
+    waves_ready()
+
+    @pl.loop(0, TICKS)
+    def _(tick):
+        moves(tick)
+
+        @pl.when(tick < CHUNKS)
         def _():
             @pl.loop(0, SPAN)
             def _(i):
-                build(turn * SPAN + i)
-
-        @pl.when(turn > FAR)
+                build(tick * SPAN + i)
+
+        @pl.when(tick == READY)
         def _():
-            for relative in range(3):
-                scatter(relative)
-
-        @pl.when(turn >= FAR)
+            remote(extra.at[pl.ds(0, CHIPS)], extra_send, extra_share, mate).wait_recv()
+
+        @pl.when(tick >= READY)
         def _():
-            chunk = turn - FAR
-            bulk(CHUNKS, share_send, share_recv.at[chunk]).wait_recv()
-            spots(chunk)
+            step = tick - READY
+            chunk = lax.div(step, 2)
+            pair = lax.rem(step, 2)
+
+            @pl.when((step >= 2) & (pair == 0))
+            def _():
+                slot = lax.rem(chunk + 1, 2)
+                scatter(0, slot)
+                scatter(1, slot)
+
+            @pl.when((step >= 2) & (pair == 1))
+            def _():
+                scatter(2, lax.rem(chunk + 1, 2))
+
+            @pl.when(pair == 0)
+            def _():
+                shared(chunk)
+
+            correlate(chunk, pair, lax.rem(chunk, 2))
+
+    for relative in range(3):
+        scatter(relative, CHUNKS % 2)
+    shared(CHUNKS - 1)
+
+    @pl.loop(0, 2)
+    def _(pair):
+        correlate(CHUNKS - 1, pair, 1 - CHUNKS % 2)
 
     def side(direction, piece):
         step = REGIONS - 1 if direction == 0 else 1
@@ -310,11 +374,11 @@
         )
 
     for direction in range(2):
-        scatter(2 * direction)
+        scatter(2 * direction, 1 - CHUNKS % 2)
         outgo[direction] = total[pl.ds(512 * direction, 256), :].astype(jnp.bfloat16)
         for piece in range(PIECES):
             side(direction, piece).start()
-    scatter(1)
+    scatter(1, 1 - CHUNKS % 2)
 
     def spread(piece, slot):
         order = piece * 2 + slot // 2
@@ -353,8 +417,9 @@
     here = pl.ds(pl.multiple_of((14 + core) * ROWS_DEV, ROWS_DEV), ROWS_DEV)
     gathered[block] = part[here]
 
-    bulk(CHUNKS * 7, ring_send, share_recv.at[0]).wait_send()
-    bulk(CHUNKS * 8, share_send, share_recv.at[0]).wait_send()
+    remote(bank.at[pl.ds(0, 7)], ring_send, share_recv.at[0], mate).wait_send()
+    remote(bank.at[pl.ds(0, 8)], share_send, share_recv.at[0], mate).wait_send()
+    remote(extra.at[pl.ds(0, 15)], extra_send, extra_share, mate).wait_send()
     for direction in range(2):
         for piece in range(PIECES):
             side(direction, piece).wait_send()
@@ -400,15 +465,17 @@
         in_specs=[pl.BlockSpec(memory_space=pltpu.VMEM)] * 3,
         out_specs=pl.BlockSpec(memory_space=pltpu.VMEM),
         scratch_shapes=[
-            pltpu.VMEM((BLOCKS, STATIONS * CAP, DEPTH), bf16),
+            pltpu.VMEM((BLOCKS, CHUNKS, 7 * SPAN * CAP // 2, 128), bf16),
+            pltpu.VMEM((BLOCKS, 16, 128), bf16),
+            pltpu.VMEM((STATIONS * CAP, 128), f32),
             pltpu.VMEM((STATIONS, DEPTH, LAGS), bf16),
             pltpu.VMEM((6, STATIONS * 3 * 16, 128), f32),
             pltpu.VMEM((6, STATIONS * 3, 128), f32),
             pltpu.VMEM((STATIONS * 3, 256), bf16),
             pltpu.VMEM((STATIONS * 3, 256), bf16),
             pltpu.VMEM((STATIONS, LAGS), f32),
-            pltpu.VMEM((SPAN * SLOTS, LAGS), bf16),
-            pltpu.VMEM((SPAN, 8, SLOTS), jnp.int32),
+            pltpu.VMEM((2, SPAN * SLOTS, LAGS), bf16),
+            pltpu.VMEM((2, SPAN, 8, SLOTS), jnp.int32),
             pltpu.VMEM((768, LAGS), f32),
             pltpu.VMEM((2, 256, LAGS), bf16),
             pltpu.VMEM((2, 256, LAGS), bf16),
@@ -416,9 +483,12 @@
             pltpu.VMEM((BLOCKS, ROWS_DEV, LAGS), bf16),
             dma((2,)),
             dma,
-            dma((2, CHUNKS, FAR)),
+            dma((CHUNKS, FAR)),
             dma,
             dma((CHUNKS,)),
+            dma,
+            dma((FAR,)),
+            dma,
             dma((2, PIECES)),
             dma((2, PIECES)),
             dma((BLOCKS,)),

time: 65.8 us -> 61.4 us (0.933)
  Pallas kernels: 63.9 us -> 59.5 us
    pallas_call x1, Pallas kernels: 63.9 us -> 59.5 us  [on_device(): pl.pallas_call(kernel, out_shape=jax.ShapeDtypeStruct((ROWS_DEV, BLOCKS *...]
where the time goes in v4:
time: 61.4 us; the launch traced here: 61.3 us
  Pallas kernels  59.5 us (97%)
  other arithmetic  1.78 us (3%)
    pallas_call x1, Pallas kernels, on_device(): pl.pallas_call(kernel, out_shape=jax.ShapeDtypeStruct((ROWS_DEV, BLOCKS *...  59.5 us
    convert_element_type x1, other arithmetic, on_device(): return result.astype(jnp.float32)  1.78 us

profile of v4, /device:TPU:1, one launch (start us, length us, event | category | flops | bytes accessed | tf_op | source)
XLA Modules:
  0.0 61.3 jit_solution(8528093932416611000)
XLA Ops:
  0.0 59.5 %shard_map.37 = bf16[16,8192]{1,0:T(8,128)(2,1)} custom-call(f32[96,512]{1,0:T(8,128)} %bitcast.6, bf16[256,450]{1,0:T(8,128)(2,1)} %bitcast.5, s32[8,32]{1,0:T(8,128)} %bitcast.7), custom_call_target="tpu_custom_call" | custom-call | tf_op jit(solution)/shard_map/pallas_call | solution.py:462
  59.5 1.8 %convert_element_type.3 = f32[16,8192]{1,0:T(8,128)} convert(bf16[16,8192]{1,0:T(8,128)(2,1)} %shard_map.37) | non-fusion elementwise | flops 131072 | bytes 786432 | tf_op jit(solution)/shard_map/convert_element_type | solution.py:501

commit v5 on v4

--- a/solution.py
+++ b/solution.py
@@ -19,17 +19,22 @@
 SLOTS = 128
 CHUNKS = 8
 SPAN = STATIONS // CHUNKS
-AHEAD = 3
+AHEAD = 5
 CHIPS = 8
 BLOCKS = 16
 REGIONS = 16
 FAR = 4
-WHEN = (1, 4, 7, 10)
-READY = WHEN[-1] + 1
-TICKS = READY + 2 * (CHUNKS - 1)
-PIECES = 4
+WHEN = (0, 2, 4, 6)
+BUILDS = (5, 5, 5, 5, 6, 6)
+PIECES = 8
 PIECE = 256 // PIECES
 MESH = pl.DeviceIdType.MESH
+
+
+def when(condition):
+    if isinstance(condition, bool):
+        return lambda body: body() if condition else None
+    return pl.when(condition)
 
 
 def kernel(
@@ -171,15 +176,21 @@
     lower = lax.broadcasted_iota(jnp.int32, (16, LAGS), 0)
 
     def build(station):
-        rolled = []
+        rolled, moved = [], {}
         for c in range(3):
             rows = pl.ds(pl.multiple_of((c * STATIONS + station) * 16, 16), 16)
-            rolled.append(jnp.concatenate([shifts[tile, rows, :] for tile in range(6)], axis=1))
+            every = jnp.concatenate([shifts[tile, rows, :] for tile in range(6)], axis=1)
+            rolled.append(every)
 
         def taken(channel, start):
-            if start == 0:
-                return rolled[channel][:, :LAGS]
-            return pltpu.roll(rolled[channel], (WIDE - start) % WIDE, 1)[:, :LAGS]
+            whole, lanes = divmod(start, 128)
+            if (channel, lanes) not in moved:
+                value = rolled[channel]
+                moved[channel, lanes] = pltpu.roll(value, WIDE - lanes, 1) if lanes else value
+            value = moved[channel, lanes]
+            if whole < 0:
+                return jnp.concatenate([value[:, WIDE - 128 :], value[:, : LAGS - 128]], axis=1)
+            return value[:, whole * 128 : whole * 128 + LAGS]
 
         for tile in range(DEPTH // 16):
             first = tile * 16
@@ -211,7 +222,7 @@
             tiles.append([bank[b, chunk, rows, :].astype(jnp.float32) for b in range(BLOCKS)])
         rows = pl.ds(3 * SPAN * CAP, 16)
         ends = [bank[b, chunk, rows, :].astype(jnp.float32) for b in range(BLOCKS)]
-        ends = jnp.concatenate([jnp.where(pair == 0, x[:8], x[8:]) for x in ends], axis=0)
+        ends = jnp.concatenate([x[pair * 8 : pair * 8 + 8] for x in ends], axis=0)
         extras = jnp.concatenate([extra[b].astype(jnp.float32)[:8] for b in range(BLOCKS)], axis=0)
         for i in range(2):
             station = chunk * SPAN + pair * 2 + i
@@ -262,103 +273,86 @@
             selector, corr[slot], preferred_element_type=jnp.float32
         )
 
-    def pair_of(ref, count):
-        return ref.at[0, pl.ds(0, count)]
-
-    def moves(tick):
+    def moves(turn):
         for hop in range(FAR):
-            late = tick - WHEN[hop]
-
-            @pl.when((late >= 0) & (late < 2 * CHUNKS) & (lax.rem(late + 2 * TICKS, 2) == 0))
+            chunk = turn - WHEN[hop]
+
+            @when((chunk >= 0) & (chunk < CHUNKS))
             def _():
-                chunk = lax.div(late, 2)
+                odd = chunk % 2 if isinstance(chunk, int) else lax.rem(chunk, 2)
                 count = 2 if hop < FAR - 1 else 1
                 arrived = bank.at[0, pl.ds(0, count)]
                 remote(arrived, ring_send, ring_recv.at[chunk, hop], mate).wait_recv()
-                for way in range(2):
-                    origin = z + (-1 if way == 0 else 1) * (hop + 1)
-                    if hop + 1 < FAR - 1:
-                        ring(way, chunk, hop + 1, origin)
-                        share(chunk, origin)
-                    elif hop + 1 == FAR - 1:
-
-                        @pl.when(lax.rem(chunk, 2) == way)
-                        def _():
-                            ring(way, chunk, hop + 1, origin)
-
-                        share(chunk, origin)
                 if hop == FAR - 1:
                     share(chunk, z + FAR)
-
-            if hop < FAR - 1:
-
-                @pl.when(tick == WHEN[hop])
-                def _():
-                    remote(extra.at[pl.ds(0, 2)], extra_send, extra_recv.at[hop], mate).wait_recv()
+                else:
+                    origins = [z - hop - 1, z + hop + 1]
+                    for way in range(2):
+
+                        @when(True if hop + 1 < FAR - 1 else odd == way)
+                        def _():
+                            ring(way, chunk, hop + 1, origins[way])
+
+                    for way in range(2):
+                        share(chunk, origins[way])
+
+            if isinstance(turn, int) and turn == WHEN[hop]:
+                count = 2 if hop < FAR - 1 else 1
+                arrived = extra.at[pl.ds(0, count)]
+                remote(arrived, extra_send, extra_recv.at[hop], mate).wait_recv()
+                if hop == FAR - 1:
+                    share_extra(z + FAR)
+                else:
                     for way in range(2):
                         origin = z + (-1 if way == 0 else 1) * (hop + 1)
                         if hop + 1 < FAR - 1 or way == 0:
                             ring_extra(way, hop + 1, origin)
                         share_extra(origin)
 
-            else:
-
-                @pl.when(tick == WHEN[hop])
-                def _():
-                    remote(extra.at[0], extra_send, extra_recv.at[hop], mate).wait_recv()
-                    share_extra(z + FAR)
-
-        @pl.when((tick > 0) & (lax.rem(tick, 2) == 0) & (lax.div(tick, 2) + AHEAD < CHUNKS))
-        def _():
-            inject(lax.div(tick, 2) + AHEAD)
-
     def shared(chunk):
         remote(bank.at[pl.ds(0, CHIPS), 0], share_send, share_recv.at[chunk], mate).wait_recv()
 
     waves_ready()
 
-    @pl.loop(0, TICKS)
-    def _(tick):
-        moves(tick)
-
-        @pl.when(tick < CHUNKS)
-        def _():
-            @pl.loop(0, SPAN)
-            def _(i):
-                build(tick * SPAN + i)
-
-        @pl.when(tick == READY)
-        def _():
-            remote(extra.at[pl.ds(0, CHIPS)], extra_send, extra_share, mate).wait_recv()
-
-        @pl.when(tick >= READY)
-        def _():
-            step = tick - READY
-            chunk = lax.div(step, 2)
-            pair = lax.rem(step, 2)
-
-            @pl.when((step >= 2) & (pair == 0))
-            def _():
-                slot = lax.rem(chunk + 1, 2)
-                scatter(0, slot)
-                scatter(1, slot)
-
-            @pl.when((step >= 2) & (pair == 1))
-            def _():
-                scatter(2, lax.rem(chunk + 1, 2))
-
-            @pl.when(pair == 0)
-            def _():
-                shared(chunk)
-
-            correlate(chunk, pair, lax.rem(chunk, 2))
-
-    for relative in range(3):
+    built = 0
+    for turn in range(WHEN[-1]):
+        moves(turn)
+        if turn and turn + AHEAD < CHUNKS:
+            inject(turn + AHEAD)
+        many = BUILDS[turn]
+
+        @pl.loop(built, built + many)
+        def _(station):
+            build(station)
+
+        built += many
+
+    def whole(chunk):
+        slot = lax.rem(chunk, 2)
+        scatter(0, slot)
+        scatter(1, slot)
+        scatter(2, slot)
+
+    moves(WHEN[-1])
+    remote(extra.at[pl.ds(0, CHIPS)], extra_send, extra_share, mate).wait_recv()
+    shared(0)
+    correlate(0, 0, 0)
+
+    @pl.loop(1, CHUNKS - 1)
+    def _(chunk):
+        moves(WHEN[-1] + chunk)
+        correlate(chunk - 1, 1, lax.rem(chunk + 1, 2))
+        whole(chunk - 1)
+        shared(chunk)
+        correlate(chunk, 0, lax.rem(chunk, 2))
+
+    moves(WHEN[-1] + CHUNKS - 1)
+    correlate(CHUNKS - 2, 1, CHUNKS % 2)
+    for relative in (0, 2):
         scatter(relative, CHUNKS % 2)
     shared(CHUNKS - 1)
 
-    @pl.loop(0, 2)
-    def _(pair):
+    for pair in range(2):
         correlate(CHUNKS - 1, pair, 1 - CHUNKS % 2)
 
     def side(direction, piece):
@@ -378,10 +372,11 @@
         outgo[direction] = total[pl.ds(512 * direction, 256), :].astype(jnp.bfloat16)
         for piece in range(PIECES):
             side(direction, piece).start()
+    scatter(1, CHUNKS % 2)
     scatter(1, 1 - CHUNKS % 2)
 
     def spread(piece, slot):
-        order = piece * 2 + slot // 2
+        order = piece * (CHIPS // PIECES) + slot // 2
         apart = 4 + order // 2 if order % 2 == 0 else 3 - order // 2
         return order, apart, slot % 2
 
@@ -403,7 +398,7 @@
         summed = total[pl.ds(256 + piece * PIECE, PIECE), :]
         summed = summed + income[0, span].astype(jnp.float32) + income[1, span].astype(jnp.float32)
         part[span] = summed.astype(jnp.bfloat16)
-        for slot in range(4):
+        for slot in range(BLOCKS // PIECES):
             order, apart, which = spread(piece, slot)
             if apart == 0:
 
@@ -435,7 +430,7 @@
         )
 
     for piece in range(PIECES):
-        for slot in range(4):
+        for slot in range(BLOCKS // PIECES):
             order, apart, which = spread(piece, slot)
             if apart == 0:
 

time: 61.4 us -> 56.9 us (0.927)
  Pallas kernels: 59.5 us -> 55 us
    pallas_call x1, Pallas kernels: 59.5 us -> 55 us  [on_device(): pl.pallas_call(kernel, out_shape=jax.ShapeDtypeStruct((ROWS_DEV, BLOCKS *...]
where the time goes in v5:
time: 56.9 us; the launch traced here: 56.8 us
  Pallas kernels  55 us (97%)
  other arithmetic  1.78 us (3%)
    pallas_call x1, Pallas kernels, on_device(): pl.pallas_call(kernel, out_shape=jax.ShapeDtypeStruct((ROWS_DEV, BLOCKS *...  55 us
    convert_element_type x1, other arithmetic, on_device(): return result.astype(jnp.float32)  1.78 us

profile of v5, /device:TPU:1, one launch (start us, length us, event | category | flops | bytes accessed | tf_op | source)
XLA Modules:
  0.0 56.8 jit_solution(15215638629834350368)
XLA Ops:
  0.0 55.0 %shard_map.37 = bf16[16,8192]{1,0:T(8,128)(2,1)} custom-call(f32[96,512]{1,0:T(8,128)} %bitcast.6, bf16[256,450]{1,0:T(8,128)(2,1)} %bitcast.5, s32[8,32]{1,0:T(8,128)} %bitcast.7), custom_call_target="tpu_custom_call" | custom-call | tf_op jit(solution)/shard_map/pallas_call | solution.py:457
  55.0 1.8 %convert_element_type.3 = f32[16,8192]{1,0:T(8,128)} convert(bf16[16,8192]{1,0:T(8,128)(2,1)} %shard_map.37) | non-fusion elementwise | flops 131072 | bytes 786432 | tf_op jit(solution)/shard_map/convert_element_type | solution.py:496

commit v6 on v5

--- a/solution.py
+++ b/solution.py
@@ -19,13 +19,13 @@
 SLOTS = 128
 CHUNKS = 8
 SPAN = STATIONS // CHUNKS
-AHEAD = 5
+AHEAD = 3
 CHIPS = 8
 BLOCKS = 16
 REGIONS = 16
 FAR = 4
 WHEN = (0, 2, 4, 6)
-BUILDS = (5, 5, 5, 5, 6, 6)
+BUILDS = (4, 4, 6, 6, 6, 6)
 PIECES = 8
 PIECE = 256 // PIECES
 MESH = pl.DeviceIdType.MESH
@@ -328,7 +328,7 @@
         built += many
 
     def whole(chunk):
-        slot = lax.rem(chunk, 2)
+        slot = chunk % 2
         scatter(0, slot)
         scatter(1, slot)
         scatter(2, slot)
@@ -338,13 +338,12 @@
     shared(0)
     correlate(0, 0, 0)
 
-    @pl.loop(1, CHUNKS - 1)
-    def _(chunk):
+    for chunk in range(1, CHUNKS - 1):
         moves(WHEN[-1] + chunk)
-        correlate(chunk - 1, 1, lax.rem(chunk + 1, 2))
+        correlate(chunk - 1, 1, (chunk + 1) % 2)
         whole(chunk - 1)
         shared(chunk)
-        correlate(chunk, 0, lax.rem(chunk, 2))
+        correlate(chunk, 0, chunk % 2)
 
     moves(WHEN[-1] + CHUNKS - 1)
     correlate(CHUNKS - 2, 1, CHUNKS % 2)

time: 56.9 us -> 56.4 us (level)
  no operation moved by 1% of the time
where the time goes in v6:
time: 56.4 us; the launch traced here: 56.2 us
  Pallas kernels  54.5 us (97%)
  other arithmetic  1.78 us (3%)
    pallas_call x1, Pallas kernels, on_device(): pl.pallas_call(kernel, out_shape=jax.ShapeDtypeStruct((ROWS_DEV, BLOCKS *...  54.5 us
    convert_element_type x1, other arithmetic, on_device(): return result.astype(jnp.float32)  1.78 us

profile of v6, /device:TPU:1, one launch (start us, length us, event | category | flops | bytes accessed | tf_op | source)
XLA Modules:
  0.0 56.2 jit_solution(18407170130947893733)
XLA Ops:
  0.0 54.5 %shard_map.37 = bf16[16,8192]{1,0:T(8,128)(2,1)} custom-call(f32[96,512]{1,0:T(8,128)} %bitcast.6, bf16[256,450]{1,0:T(8,128)(2,1)} %bitcast.5, s32[8,32]{1,0:T(8,128)} %bitcast.7), custom_call_target="tpu_custom_call" | custom-call | tf_op jit(solution)/shard_map/pallas_call | solution.py:456
  54.5 1.8 %convert_element_type.3 = f32[16,8192]{1,0:T(8,128)} convert(bf16[16,8192]{1,0:T(8,128)(2,1)} %shard_map.37) | non-fusion elementwise | flops 131072 | bytes 786432 | tf_op jit(solution)/shard_map/convert_element_type | solution.py:495

commit v7 on v6

--- a/solution.py
+++ b/solution.py
@@ -446,6 +446,10 @@
 
     for source in range(BLOCKS):
         out_ref[:, pl.ds(source * LAGS, LAGS)] = gathered[source]
+
+
+def widen(narrow_ref, wide_ref):
+    wide_ref[...] = narrow_ref[...].astype(jnp.float32)
 
 
 def on_device(waveforms, templates, pair_rows):
@@ -492,7 +496,12 @@
             collective_id=0, has_side_effects=True, vmem_limit_bytes=60 * 1024 * 1024
         ),
     )(waves, own, pair_rows.T)
-    return result.astype(jnp.float32)
+    return pl.pallas_call(
+        widen,
+        out_shape=jax.ShapeDtypeStruct((ROWS_DEV, BLOCKS * LAGS), f32),
+        in_specs=[pl.BlockSpec(memory_space=pltpu.VMEM)],
+        out_specs=pl.BlockSpec(memory_space=pltpu.VMEM),
+    )(result)
 
 
 def solution(mesh):

time: 56.4 us -> 56.4 us (level)
  other arithmetic: 1.78 us -> 0 us
  Pallas kernels: 54.5 us -> 56.2 us
    convert_element_type x1 -> x0, other arithmetic: 1.78 us -> none  [on_device(): return result.astype(jnp.float32)]
    pallas_call x0 -> x1, Pallas kernels: none -> 1.78 us  [on_device(): pl.pallas_call(widen, out_shape=jax.ShapeDtypeStruct((ROWS_DEV, BLOCKS *...]
where the time goes in v7:
time: 56.4 us; the launch traced here: 56.2 us
  Pallas kernels  56.2 us (100%)
    pallas_call x1, Pallas kernels, on_device(): pl.pallas_call(kernel, out_shape=jax.ShapeDtypeStruct((ROWS_DEV, BLOCKS *...  54.5 us
    pallas_call x1, Pallas kernels, on_device(): pl.pallas_call(widen, out_shape=jax.ShapeDtypeStruct((ROWS_DEV, BLOCKS *...  1.78 us

profile of v7, /device:TPU:1, one launch (start us, length us, event | category | flops | bytes accessed | tf_op | source)
XLA Modules:
  0.0 56.2 jit_solution(12025033991321618926)
XLA Ops:
  0.0 54.5 %shard_map.37.narrow_ref = bf16[16,8192]{1,0:T(8,128)(2,1)} custom-call(f32[96,512]{1,0:T(8,128)} %bitcast.6, bf16[256,450]{1,0:T(8,128)(2,1)} %bitcast.5, s32[8,32]{1,0:T(8,128)} %bitcast.7), custom_call_target="tpu_custom_call" | custom-call | tf_op jit(solution)/shard_map/pallas_call | solution.py:460
  54.5 1.8 %shard_map.38 = f32[16,8192]{1,0:T(8,128)} custom-call(bf16[16,8192]{1,0:T(8,128)(2,1)} %shard_map.37.narrow_ref), custom_call_target="tpu_custom_call" | custom-call | tf_op jit(solution)/shard_map/pallas_call | solution.py:499
